TPU v7x, 128 devices: a whole 4x4x4 slice. The times are simulated.
128 devices in a mesh: dp: 4 (over x), expert: 32 (over z, y, core).
Axes of the slice: x: 4, y: 4, z: 4, core: 2. Of those that a mesh axis runs over, the one named last changes fastest.
Arguments:
- tokens: bfloat16 [16384, 7168], P(('dp', 'expert')), may hold values from -6 to 6
- out_grad: bfloat16 [16384, 7168], P(('dp', 'expert')), may hold values from -3 to 3
- expert_ids: int32 [16384, 1], P(('dp', 'expert')), may hold values from 0 to 31; in each aligned block of 128 rows (0 to 127, 128 to 255, ...) at most 6 rows name the same one
- route_probs: float32 [16384, 1], P(('dp', 'expert')), may hold values from 0.2 to 1
- w_gate: bfloat16 [32, 7168, 1024], P('expert', None, 'dp'), may hold values from -0.0625 to 0.0625
- w_up: bfloat16 [32, 7168, 1024], P('expert', None, 'dp'), may hold values from -0.0625 to 0.0625
- w_down: bfloat16 [32, 1024, 7168], P('expert', 'dp'), may hold values from -0.1875 to 0.1875
Outputs:
- token_grad: bfloat16 [16384, 7168], P(('dp', 'expert'))
- gate_grad: bfloat16 [32, 7168, 1024], P('expert', None, 'dp')
- up_grad: bfloat16 [32, 7168, 1024], P('expert', None, 'dp')
Inputs may be any that keep to these rules, and one draw needn't show every extreme that they name: `expert_ids`: in the rows of one device (aligned blocks of 128 rows) no expert is named more than 6 times, a bound that some block reaches.
All inputs are finite; a program needn't handle non-finite values.
Results may differ from a plain program's by a relative error of at most 0.0064.
Values may be sent and summed in bfloat16 or wider, within the bound.
A program may use at most 192 MiB of HBM per device.

v0:
```python
import jax
import jax.numpy as jnp
from jax import lax
from jax.sharding import PartitionSpec as P


def route_tables(expert_ids, experts, capacity):
    flat_ids = expert_ids.reshape(-1)
    labels = lax.broadcasted_iota(jnp.int32, (1, experts), 1)
    onehot = (flat_ids[:, None] == labels).astype(jnp.int32)
    slot_rank = jnp.sum((jnp.cumsum(onehot, axis=0) - 1) * onehot, axis=1)
    slot_ids = flat_ids * capacity + slot_rank
    positions = lax.broadcasted_iota(jnp.int32, (experts * capacity, 1), 0)
    return (positions == slot_ids[None, :]).astype(jnp.bfloat16)


def hidden_grads(x_rows, y_rows, gate_w, up_w, down_w):
    gate_val = jnp.dot(x_rows, gate_w, preferred_element_type=jnp.float32)
    up_val = jnp.dot(x_rows, up_w, preferred_element_type=jnp.float32)
    hidden_grad = lax.dot_general(
        y_rows, down_w, (((1,), (1,)), ((), ())), preferred_element_type=jnp.float32
    )
    sigmoid_val = jax.nn.sigmoid(gate_val)
    grad_up = (hidden_grad * gate_val * sigmoid_val).astype(jnp.bfloat16)
    grad_gate = (
        hidden_grad * up_val * sigmoid_val * (1.0 + gate_val * (1.0 - sigmoid_val))
    ).astype(jnp.bfloat16)
    return (grad_gate, grad_up)


def contract_rows(x_rows, grads):
    return lax.dot_general(
        x_rows, grads, (((0,), (0,)), ((), ())), preferred_element_type=jnp.float32
    )


def back_rows(stored_rows, gate_w, up_w, quarter):
    partial_value = lax.dot_general(
        stored_rows[:, :quarter],
        gate_w,
        (((1,), (1,)), ((), ())),
        preferred_element_type=jnp.float32,
    )
    return partial_value + lax.dot_general(
        stored_rows[:, quarter:], up_w, (((1,), (1,)), ((), ())), preferred_element_type=jnp.float32
    )


def local(tokens, out_grad, expert_ids, route_probs, w_gate, w_up, w_down):
    experts = lax.axis_size("expert")
    groups = lax.axis_size("dp")
    tok_count, model_width = tokens.shape
    route_count = expert_ids.shape[1]
    capacity = max(2, 3 * tok_count * route_count // (2 * experts))
    placement = route_tables(expert_ids, experts, capacity)
    tok_rep = jnp.repeat(tokens, route_count, axis=0)
    scaled = (
        jnp.repeat(out_grad, route_count, axis=0).astype(jnp.float32)
        * route_probs.reshape(-1)[:, None]
    ).astype(jnp.bfloat16)
    send_x = jnp.dot(placement, tok_rep, preferred_element_type=jnp.float32).astype(jnp.bfloat16)
    send_y = jnp.dot(placement, scaled, preferred_element_type=jnp.float32).astype(jnp.bfloat16)
    gate_w = w_gate[0]
    up_w = w_up[0]
    down_w = w_down[0]
    quarter = gate_w.shape[1]
    own_rows = experts * capacity
    copies_x = jnp.tile(send_x, (groups, 1))
    copies_y = jnp.tile(send_y, (groups, 1))
    received_x, received_y = (
        lax.all_to_all(copies_x, ("dp", "expert"), split_axis=0, concat_axis=0, tiled=True),
        lax.all_to_all(copies_y, ("dp", "expert"), split_axis=0, concat_axis=0, tiled=True),
    )
    grad_gate, grad_up = hidden_grads(received_x, received_y, gate_w, up_w, down_w)
    acc_gate = contract_rows(received_x, grad_gate)
    acc_up = contract_rows(received_x, grad_up)
    joined = jnp.concatenate((grad_gate, grad_up), axis=1)
    state_now = (acc_gate, acc_up, joined)
    acc_gate, acc_up, stored = state_now
    pieces_out = back_rows(stored, gate_w, up_w, quarter).astype(jnp.bfloat16)
    received = lax.all_to_all(pieces_out, ("dp", "expert"), split_axis=0, concat_axis=0, tiled=True)
    rows_back = jnp.sum(
        received.reshape(groups, own_rows, model_width).astype(jnp.float32), axis=0
    ).astype(jnp.bfloat16)
    route_grads = lax.dot_general(
        placement, rows_back, (((0,), (0,)), ((), ())), preferred_element_type=jnp.float32
    )
    token_grad = jnp.sum(route_grads.reshape(tok_count, route_count, model_width), axis=1).astype(
        jnp.bfloat16
    )
    return (token_grad, acc_gate.astype(jnp.bfloat16)[None], acc_up.astype(jnp.bfloat16)[None])


def solution(mesh):
    in_specs = (
        P(("dp", "expert"), None),
        P(("dp", "expert"), None),
        P(("dp", "expert"), None),
        P(("dp", "expert"), None),
        P("expert", None, "dp"),
        P("expert", None, "dp"),
        P("expert", "dp", None),
    )
    out_specs = (P(("dp", "expert"), None), P("expert", None, "dp"), P("expert", None, "dp"))
    return jax.shard_map(local, mesh=mesh, in_specs=in_specs, out_specs=out_specs, check_vma=False)
```

profile of v0, /device:TPU:1, one launch (start us, length us, event | category | flops | bytes accessed | tf_op | source)
XLA Modules:
  0.0 762.9 jit_solution(10861592596128236631)
XLA Ops:
  0.6 0.0 copy-start
  0.6 0.9 fusion.24
  1.5 0.2 reduce_window_sum.11
  1.7 0.8 select_reduce_fusion
  2.5 0.7 multiply_add_fusion
  3.2 0.0 copy-done
  3.2 2.4 convolution_convert_fusion.2
  5.6 7.3 tile.5
  12.9 15.9 %all_to_all.25 = bf16[128,6,7168]{2,1,0:T(8,128)(2,1)} reshape(bf16[4,192,7168]{2,1,0:T(8,128)(2,1)} %tile.5) | data formatting | bytes 22020096 | tf_op jit(solution)/shard_map/all_to_all | solution.py:71
  28.8 0.0 copy-start.4
  28.8 0.0 copy-start.5
  28.8 11.9 %all-to-all-start.1 = ((bf16[128,6,7168]{2,1,0:T(8,128)(2,1)}), bf16[128,6,7168]{2,1,0:T(8,128)(2,1)}, u32[]{:S(2)}, u32[]{:S(2)}) async-start(bf16[128,6,7168]{2,1,0:T(8,128)(2,1)} %all_to_all.25), calls=%async_computation.1 | async-start | bytes 29360128 | tf_op jit(solution)/shard_map/all_to_all | solution.py:71
  40.7 0.0 copy-done.4
  40.7 0.0 copy-done.5
  40.8 2.5 convolution_convert_fusion.3
  43.3 7.2 tile.4
  50.5 15.2 %all_to_all.22 = bf16[128,6,7168]{2,1,0:T(8,128)(2,1)} reshape(bf16[4,192,7168]{2,1,0:T(8,128)(2,1)} %tile.4) | data formatting | bytes 22020096 | tf_op jit(solution)/shard_map/all_to_all | solution.py:72
  65.7 174.7 %all-to-all-done.1 = bf16[128,6,7168]{2,1,0:T(8,128)(2,1)} async-done(((bf16[128,6,7168]{2,1,0:T(8,128)(2,1)}), bf16[128,6,7168]{2,1,0:T(8,128)(2,1)}, u32[]{:S(2)}, u32[]{:S(2)}) %all-to-all-start.1) | async-done | bytes 11010080 | tf_op jit(solution)/shard_map/all_to_all | solution.py:71
  240.4 12.2 %all-to-all-start = ((bf16[128,6,7168]{2,1,0:T(8,128)(2,1)}), bf16[128,6,7168]{2,1,0:T(8,128)(2,1)}, u32[]{:S(2)}, u32[]{:S(2)}) async-start(bf16[128,6,7168]{2,1,0:T(8,128)(2,1)} %all_to_all.22), calls=%async_computation | async-start | bytes 29360128 | tf_op jit(solution)/shard_map/all_to_all | solution.py:72
  252.6 16.4 %all_to_all.27 = bf16[768,7168]{1,0:T(8,128)(2,1)} reshape(bf16[128,6,7168]{2,1,0:T(8,128)(2,1)} %all-to-all-done.1) | data formatting | bytes 22020096 | tf_op jit(solution)/shard_map/all_to_all | solution.py:71
  269.0 6.9 fusion.4
  275.9 173.8 %all-to-all-done = bf16[128,6,7168]{2,1,0:T(8,128)(2,1)} async-done(((bf16[128,6,7168]{2,1,0:T(8,128)(2,1)}), bf16[128,6,7168]{2,1,0:T(8,128)(2,1)}, u32[]{:S(2)}, u32[]{:S(2)}) %all-to-all-start) | async-done | bytes 11010080 | tf_op jit(solution)/shard_map/all_to_all | solution.py:72
  449.7 16.5 %all_to_all.24 = bf16[768,7168]{1,0:T(8,128)(2,1)} reshape(bf16[128,6,7168]{2,1,0:T(8,128)(2,1)} %all-to-all-done) | data formatting | bytes 22020096 | tf_op jit(solution)/shard_map/all_to_all | solution.py:72
  466.2 0.0 copy-start.2
  466.2 7.1 multiply_convert_fusion.2
  473.3 0.0 copy-done.2
  473.3 0.0 copy-start.3
  473.3 7.4 fusion.21
  480.7 0.0 copy-done.3
  480.7 9.2 %fusion.2 = f32[768,7168]{1,0:T(8,128)} fusion(bf16[768,256]{1,0:T(8,128)(2,1)S(1)} %fusion.21, bf16[1,7168,256]{2,1,0:T(8,128)(2,1)S(1)} %copy-done.3), kind=kOutput, calls=%fused_computation.8 | convolution fusion | flops 2818572288 | bytes 26083328 | tf_op jit(solution)/shard_map/dot_general | solution.py:38
  489.9 13.2 %add_convert_fusion = bf16[768,7168]{1,0:T(8,128)(2,1)} fusion(f32[768,7168]{1,0:T(8,128)} %fusion.2, bf16[768,256]{1,0:T(8,128)(2,1)S(1)} %get-tuple-element.3, bf16[1,7168,256]{2,1,0:T(8,128)(2,1)} %param.12), kind=kOutput, calls=%fused_computation | convolution fusion | flops 2829582336 | bytes 37093376 | tf_op jit(solution)/shard_map/dot_general | solution.py:44
  503.2 15.9 %all_to_all.28 = bf16[128,6,7168]{2,1,0:T(8,128)(2,1)} reshape(bf16[768,7168]{1,0:T(8,128)(2,1)} %add_convert_fusion) | data formatting | bytes 22020096 | tf_op jit(solution)/shard_map/all_to_all | solution.py:81
  519.1 17.8 %all-to-all-start.2 = ((bf16[128,6,7168]{2,1,0:T(8,128)(2,1)}), bf16[128,6,7168]{2,1,0:T(8,128)(2,1)}, u32[]{:S(2)}, u32[]{:S(2)}) async-start(bf16[128,6,7168]{2,1,0:T(8,128)(2,1)} %all_to_all.28), calls=%async_computation.2 | async-start | bytes 29360128 | tf_op jit(solution)/shard_map/all_to_all | solution.py:81
  536.9 9.1 %fusion = bf16[1,7168,256]{2,1,0:T(8,128)(2,1)} fusion(bf16[768,7168]{1,0:T(8,128)(2,1)} %all_to_all.27, bf16[768,256]{1,0:T(8,128)(2,1)S(1)} %fusion.21), kind=kOutput, calls=%fused_computation.5 | convolution fusion | flops 2820407296 | bytes 15073280 | tf_op jit(solution)/shard_map/dot_general | solution.py:32
  546.0 9.1 %fusion.1 = bf16[1,7168,256]{2,1,0:T(8,128)(2,1)} fusion(bf16[768,7168]{1,0:T(8,128)(2,1)} %all_to_all.27, bf16[768,256]{1,0:T(8,128)(2,1)S(1)} %get-tuple-element.3), kind=kOutput, calls=%fused_computation.6 | convolution fusion | flops 2820407296 | bytes 15073280 | tf_op jit(solution)/shard_map/dot_general | solution.py:32
  555.0 179.0 %all-to-all-done.2 = bf16[128,6,7168]{2,1,0:T(8,128)(2,1)} async-done(((bf16[128,6,7168]{2,1,0:T(8,128)(2,1)}), bf16[128,6,7168]{2,1,0:T(8,128)(2,1)}, u32[]{:S(2)}, u32[]{:S(2)}) %all-to-all-start.2) | async-done | bytes 11010080 | tf_op jit(solution)/shard_map/all_to_all | solution.py:81
  734.0 16.5 %reshape.41 = bf16[4,192,7168]{2,1,0:T(8,128)(2,1)} reshape(bf16[128,6,7168]{2,1,0:T(8,128)(2,1)} %all-to-all-done.2) | data formatting | bytes 22020096 | tf_op jit(solution)/shard_map/reshape | solution.py:83
  750.5 0.0 copy-start.1
  750.5 8.7 %reduce_sum.26 = bf16[192,7168]{1,0:T(8,128)(2,1)} reduce(bf16[4,192,7168]{2,1,0:T(8,128)(2,1)} %reshape.41, bf16[]{:T(256)} %constant.15.clone.1), dimensions={0}, to_apply=%region_2.3 | reduce | flops 4128768 | bytes 13762562 | tf_op jit(solution)/shard_map/reduce_sum | solution.py:82
  759.2 3.7 convolution_convert_fusion.4
  762.9 0.0 copy-done.1
Async XLA Ops:
  0.6 2.6 copy-start
  28.8 11.9 %copy-start.4 = (bf16[128,7168]{1,0:T(8,128)(2,1)S(1)}, bf16[128,7168]{1,0:T(8,128)(2,1)}, u32[]{:S(2)}) copy-start(bf16[128,7168]{1,0:T(8,128)(2,1)} %param.8) | copy-start | bytes 5505028
  28.8 11.9 %copy-start.5 = (f32[128,1]{0,1:T(1,128)S(1)}, f32[128,1]{0,1:T(1,128)}, u32[]{:S(2)}) copy-start(f32[128,1]{0,1:T(1,128)} %param.10) | copy-start | bytes 1540
  28.8 211.6 %all-to-all-start.1 = ((bf16[128,6,7168]{2,1,0:T(8,128)(2,1)}), bf16[128,6,7168]{2,1,0:T(8,128)(2,1)}, u32[]{:S(2)}, u32[]{:S(2)}) async-start(bf16[128,6,7168]{2,1,0:T(8,128)(2,1)} %all_to_all.25), calls=%async_computation.1 | async-start | bytes 29360128 | tf_op jit(solution)/shard_map/all_to_all | solution.py:71
  240.4 209.3 %all-to-all-start = ((bf16[128,6,7168]{2,1,0:T(8,128)(2,1)}), bf16[128,6,7168]{2,1,0:T(8,128)(2,1)}, u32[]{:S(2)}, u32[]{:S(2)}) async-start(bf16[128,6,7168]{2,1,0:T(8,128)(2,1)} %all_to_all.22), calls=%async_computation | async-start | bytes 29360128 | tf_op jit(solution)/shard_map/all_to_all | solution.py:72
  466.2 7.1 copy-start.2
  473.3 7.4 copy-start.3
  519.1 215.0 %all-to-all-start.2 = ((bf16[128,6,7168]{2,1,0:T(8,128)(2,1)}), bf16[128,6,7168]{2,1,0:T(8,128)(2,1)}, u32[]{:S(2)}, u32[]{:S(2)}) async-start(bf16[128,6,7168]{2,1,0:T(8,128)(2,1)} %all_to_all.28), calls=%async_computation.2 | async-start | bytes 29360128 | tf_op jit(solution)/shard_map/all_to_all | solution.py:81
  750.5 12.4 %copy-start.1 = (bf16[128,7168]{1,0:T(8,128)(2,1)S(1)}, bf16[128,7168]{1,0:T(8,128)(2,1)}, u32[]{:S(2)}) copy-start(bf16[128,7168]{1,0:T(8,128)(2,1)} %param.7) | copy-start | bytes 5505028
where the time goes:
time: 771 us; the launch traced here: 763 us
  waiting for transfers between devices  528 us (68%)
  local copies, waits for them, and re-layouts  111 us (14%)
  matrix products  70.5 us (9%)
  starting transfers between devices  41.9 us (5%)
  other arithmetic  11.2 us (1%)
    all_to_all x1, waiting for transfers between devices, local(): lax.all_to_all(pieces_out, ('dp', 'expert'), split_axis=0, concat_axis=0,...  179 us
    all_to_all x1, waiting for transfers between devices, local(): lax.all_to_all(copies_x, ('dp', 'expert'), split_axis=0, concat_axis=0, t...  175 us
    all_to_all x1, waiting for transfers between devices, local(): lax.all_to_all(copies_y, ('dp', 'expert'), split_axis=0, concat_axis=0, t...  174 us
    all_to_all x2, local copies, waits for them, and re-layouts, local(): lax.all_to_all(copies_x, ('dp', 'expert'), split_axis=0, concat_axis=0, t...  32.3 us
    all_to_all x2, local copies, waits for them, and re-layouts, local(): lax.all_to_all(copies_y, ('dp', 'expert'), split_axis=0, concat_axis=0, t...  31.6 us
    dot_general x2, matrix products, contract_rows(): lax.dot_general(x_rows, grads, (((0,), (0,)), ((), ())), preferred_elemen...  18.1 us
    all_to_all x1, starting transfers between devices, local(): lax.all_to_all(pieces_out, ('dp', 'expert'), split_axis=0, concat_axis=0,...  17.8 us
    reshape x1, local copies, waits for them, and re-layouts, local(): received.reshape(groups, own_rows, model_width).astype(jnp.float32)  16.5 us
  transfers between devices with their start and end apart: 3, of which 3 were waited for; matrix products, arithmetic and copies ran while one was open for 5% of the time, Pallas kernels for 0%

commit v1 on v0

v1 whole, which is shorter than its diff:
```python
import jax
import jax.numpy as jnp
from jax import lax
from jax.experimental import pallas as pl
from jax.experimental.pallas import tpu as pltpu
from jax.sharding import PartitionSpec as P

MESH = pl.DeviceIdType.MESH
F32, BF16 = jnp.float32, jnp.bfloat16
CHUNKS = 3
PER = 2
OCT = 8
SLAB = PER * OCT
X, Y = 0, 1
NN = (((1,), (0,)), ((), ()))
NT = (((1,), (1,)), ((), ()))
TN = (((0,), (0,)), ((), ()))


def dot(a, b, dims=NN):
    return lax.dot_general(a, b, dims, preferred_element_type=F32)


def iota(shape, axis):
    return lax.broadcasted_iota(jnp.int32, shape, axis)


def kernel(
    ids_col, ids_row, probs, tok_hbm, og_hbm, wg_hbm, wu_hbm, wd_hbm,
    tg_hbm, gg_hbm, ug_hbm,
    tok, q, wg, wu, wd, send, recv, rows, relay, fin, back, acc, grads, stage,
    load_sem, disp_send, disp_recv, own_sem, ag_send, ag_recv, rs_send, rs_recv,
    ret_send, ret_recv, retown_sem, out_sem,
):
    n_x = lax.axis_size("dp")
    n_e = lax.axis_size("expert")
    me_x = lax.axis_index("dp")
    me_e = lax.axis_index("expert")
    nbr = (lax.rem(me_x + 1, n_x), lax.rem(me_x + n_x - 1, n_x))
    far = lax.rem(me_x + 2, n_x)
    toks, width = tok_hbm.shape
    oct_w = width // OCT
    quarter = wg_hbm.shape[1]
    half = n_e
    gs = n_e // 2
    chunk_rows = n_x * n_e * PER
    log_half = half.bit_length() - 1

    loads = []
    for a, src in ((X, tok_hbm), (Y, og_hbm)):
        for j in range(OCT):
            loads.append(
                pltpu.make_async_copy(
                    src.at[:, pl.ds(j * oct_w, oct_w)], tok.at[a, j], load_sem.at[a, j]
                )
            )
            loads[-1].start()
    weights = [
        pltpu.make_async_copy(src, dst, load_sem.at[2, i])
        for i, (src, dst) in enumerate(((wg_hbm, wg), (wu_hbm, wu), (wd_hbm, wd)))
    ]
    for w in weights:
        w.start()

    barrier = pltpu.get_barrier_semaphore()

    def greet(d, carry):
        pl.semaphore_signal(
            barrier, inc=1, device_id=(me_x, lax.rem(me_e + d, n_e)), device_id_type=MESH
        )
        return carry

    lax.fori_loop(1, n_e, greet, 0)
    for x in nbr:
        pl.semaphore_signal(barrier, inc=1, device_id=(x, me_e), device_id_type=MESH)

    same = ids_col[...] == ids_row[...]
    first, second = iota((toks, toks), 0), iota((toks, toks), 1)
    rank_row = jnp.sum(jnp.where(same & (first < second), 1, 0), axis=0, keepdims=True)
    rank_col = jnp.sum(jnp.where(same & (second < first), 1, 0), axis=1, keepdims=True)
    key_row = ids_row[...] * PER + (rank_row & 1)
    key_col = ids_col[...] * PER + (rank_col & 1)

    n_slab_rows = n_e * SLAB
    step = min(128, n_slab_rows)

    def build_q(c):
        keyc = jnp.where((rank_row >> 1) == c, key_row, -1)
        i = iota((n_slab_rows, 1), 0)
        for j in range(OCT):
            want = jnp.where(((i >> 1) & (OCT - 1)) == j, (i >> 4) * PER + (i & 1), -2)
            q[:, j * toks : (j + 1) * toks] = jnp.where(want == keyc, 1.0, 0.0).astype(BF16)

    def fill(a, c):
        def body(m, carry):
            part = q[pl.ds(pl.multiple_of(m * step, step), step), :]
            out = dot(part, tok[a].reshape(OCT * toks, oct_w)).astype(BF16)
            send[a, c, pl.ds(m * (step // SLAB), step // SLAB)] = out.reshape(
                step // SLAB, SLAB, oct_w
            )
            return carry

        lax.fori_loop(0, n_slab_rows // step, body, 0)

    def scatter(src, dst, send_sem, recv_sem, self_sem):
        pltpu.make_async_copy(src.at[me_e], dst.at[me_e], self_sem).start()

        def body(d, carry):
            peer = lax.rem(me_e + d, n_e)
            pltpu.make_async_remote_copy(
                src_ref=src.at[peer],
                dst_ref=dst.at[me_e],
                send_sem=send_sem,
                recv_sem=recv_sem,
                device_id=(me_x, peer),
                device_id_type=MESH,
            ).start()
            return carry

        lax.fori_loop(1, n_e, body, 0)

    def scattered(src, dst, send_sem, recv_sem):
        return pltpu.make_async_remote_copy(
            src_ref=src.at[pl.ds(0, n_e - 1)],
            dst_ref=dst.at[pl.ds(0, n_e - 1)],
            send_sem=send_sem,
            recv_sem=recv_sem,
            device_id=(nbr[0], me_e),
            device_id_type=MESH,
        )

    def dispatch(a, c):
        scatter(
            send.at[a, c], recv.at[a, c], disp_send.at[a, c], disp_recv.at[a, c], own_sem.at[a, c]
        )

    def dispatched(a, c):
        return scattered(send.at[a, c], recv.at[a, c], disp_send.at[a, c], disp_recv.at[a, c])

    def hop(a, c, block, h, way, slot):
        ref = rows.at[a, c, block * 2 + h]
        return pltpu.make_async_remote_copy(
            src_ref=ref,
            dst_ref=ref,
            send_sem=ag_send.at[a, c, way, slot],
            recv_sem=ag_recv.at[a, c, way, slot],
            device_id=(nbr[way], me_e),
            device_id_type=MESH,
        )

    size = gs * SLAB

    def perm(row, col):
        j, rest = row >> log_half, row & (half - 1)
        return jnp.where(col == (rest >> 1) * SLAB + j * PER + (rest & 1), 1.0, 0.0).astype(BF16)

    def own(a, c):
        pltpu.make_async_copy(send.at[a, c, me_e], recv.at[a, c, me_e], own_sem.at[a, c]).wait()
        dispatched(a, c).wait_recv()
        order = perm(iota((size, size), 0), iota((size, size), 1))
        for h in range(2):
            block = recv[a, c, h * gs : (h + 1) * gs].reshape(size, oct_w)
            out = dot(order, block).astype(BF16)
            for j in range(OCT):
                rows[a, c, me_x * 2 + h, :, j * oct_w : (j + 1) * oct_w] = out[
                    j * half : (j + 1) * half
                ]
        hop(a, c, me_x, 0, 0, 0).start()
        hop(a, c, me_x, 1, 1, 1).start()
        hop(a, c, me_x, 1, 0, 1).start()
        hop(a, c, me_x, 0, 1, 0).start()

    def arrive(a, c):
        for way in range(2):
            block = nbr[1 - way]
            hop(a, c, block, way, way, way).wait_recv()
            hop(a, c, block, way, way, 2).start()

    def complete(a, c):
        for way in range(2):
            hop(a, c, nbr[1 - way], 1 - way, way, 1 - way).wait_recv()
            hop(a, c, far, way, way, 2).wait_recv()

    def sent(a, c):
        for way in range(2):
            for slot in range(2):
                hop(a, c, me_x, slot, way, slot).wait_send()
            hop(a, c, nbr[1 - way], way, way, 2).wait_send()

    kw = width // 4

    def forward(c):
        def body(k, carry):
            cols = pl.ds(pl.multiple_of(k * kw, 128), kw)
            x = rows[X, c, :, :, cols].reshape(chunk_rows, kw)
            g = dot(x, wg[cols, :])
            u = dot(x, wu[cols, :])

            @pl.when(k == 0)
            def _():
                acc[0] = g
                acc[1] = u

            @pl.when(k > 0)
            def _():
                acc[0] += g
                acc[1] += u

            return carry

        lax.fori_loop(0, 4, body, 0)

    bw = 512 if width % 512 == 0 else 128

    def backward(c):
        def body(k, carry):
            cols = pl.ds(pl.multiple_of(k * kw, 128), kw)
            y = rows[Y, c, :, :, cols].reshape(chunk_rows, kw)
            h = dot(y, wd[:, cols], NT)

            @pl.when(k == 0)
            def _():
                acc[2] = h

            @pl.when(k > 0)
            def _():
                acc[2] += h

            return carry

        lax.fori_loop(0, 4, body, 0)
        gate_val, up_val, hidden = acc[0], acc[1], acc[2]
        s = jax.nn.sigmoid(gate_val)
        grad_up = (hidden * gate_val * s).astype(BF16)
        grad_gate = (hidden * up_val * s * (1.0 + gate_val * (1.0 - s))).astype(BF16)
        grads[c * chunk_rows : (c + 1) * chunk_rows, :quarter] = grad_gate
        grads[c * chunk_rows : (c + 1) * chunk_rows, quarter:] = grad_up

        def part(d, carry):
            cols = pl.ds(pl.multiple_of(d * bw, 128), bw)
            g = grads[c * chunk_rows : (c + 1) * chunk_rows, :quarter]
            u = grads[c * chunk_rows : (c + 1) * chunk_rows, quarter:]
            out = dot(g, wg[cols, :], NT) + dot(u, wu[cols, :], NT)
            rows[Y, c, :, :, cols] = out.astype(BF16).reshape(2 * n_x, half, bw)
            return carry

        lax.fori_loop(0, width // bw, part, 0)

    def back_of(c):
        return (recv.at[X, 0], recv.at[Y, 0], back)[c]

    def toward(c, way, slot):
        dst_block = far if slot == 0 else nbr[way]
        h = (way, 1 - way, way)[slot]
        src = rows.at[Y, c, dst_block * 2 + h]
        dst = relay.at[c, way] if slot == 0 else fin.at[c, way, h]
        return pltpu.make_async_remote_copy(
            src_ref=src,
            dst_ref=dst,
            send_sem=rs_send.at[c, way, slot],
            recv_sem=rs_recv.at[c, way, slot],
            device_id=(nbr[way], me_e),
            device_id_type=MESH,
        )

    def start_reduce(c):
        for slot in range(2):
            for way in range(2):
                toward(c, way, slot).start()

    def pass_on(c):
        for way in range(2):
            toward(c, way, 0).wait_recv()

            def body(d, carry):
                cols = pl.ds(pl.multiple_of(d * bw, 128), bw)
                at = nbr[way] * 2 + way
                total = rows[Y, c, at, :, cols].astype(F32) + relay[c, way, :, cols].astype(F32)
                rows[Y, c, at, :, cols] = total.astype(BF16)
                return carry

            lax.fori_loop(0, width // bw, body, 0)
            toward(c, way, 2).start()

    def finish(c):
        dispatched(X, c).wait_send()
        order = perm(iota((size, size), 1), iota((size, size), 0))
        for way in range(2):
            for slot in (1, 2):
                toward(c, way, slot).wait_recv()
        for h in range(2):
            blocks = []
            for j in range(OCT):
                cols = slice(j * oct_w, (j + 1) * oct_w)
                total = (
                    rows[Y, c, me_x * 2 + h, :, cols].astype(F32)
                    + fin[c, 0, h, :, cols].astype(F32)
                    + fin[c, 1, h, :, cols].astype(F32)
                )
                blocks.append(total.astype(BF16))
            out = dot(order, jnp.concatenate(blocks, axis=0)).astype(BF16)
            send[X, c, h * gs : (h + 1) * gs] = out.reshape(gs, SLAB, oct_w)
        scatter(send.at[X, c], back_of(c), ret_send.at[c], ret_recv.at[c], retown_sem.at[c])

    def weight_grads():
        def tile(i, slot):
            cols = pl.ds(pl.multiple_of(i * bw, 128), bw)
            return [
                pltpu.make_async_copy(stage.at[slot, o], dst.at[cols, :], out_sem.at[slot, o])
                for o, dst in ((0, gg_hbm), (1, ug_hbm))
            ]

        def body(i, carry):
            slot = lax.rem(i, 2)

            @pl.when(i >= 2)
            def _():
                for copy in tile(i - 2, slot):
                    copy.wait()

            cols = pl.ds(pl.multiple_of(i * bw, 128), bw)
            x = rows[X, :, :, :, cols].reshape(CHUNKS * chunk_rows, bw)
            out = dot(x, grads[...], TN).astype(BF16)
            stage[slot, 0] = out[:, :quarter]
            stage[slot, 1] = out[:, quarter:]
            for copy in tile(i, slot):
                copy.start()
            return carry

        n = width // bw
        lax.fori_loop(0, n, body, 0)
        for i in (n - 2, n - 1):
            for copy in tile(i, i % 2):
                copy.wait()

    def token_grads():
        for c in range(CHUNKS):
            pltpu.make_async_copy(send.at[X, c, me_e], back_of(c).at[me_e], retown_sem.at[c]).wait()
            scattered(send.at[X, c], back_of(c), ret_send.at[c], ret_recv.at[c]).wait_recv()
        i = iota((1, n_slab_rows), 1)

        def body(j, carry):
            want = jnp.where(((i >> 1) & (OCT - 1)) == j, (i >> 4) * PER + (i & 1), -2)
            total = None
            for c in range(CHUNKS):
                keyc = jnp.where((rank_col >> 1) == c, key_col, -1)
                place = jnp.where(keyc == want, 1.0, 0.0).astype(BF16)
                one = dot(place, back_of(c)[...].reshape(n_slab_rows, oct_w))
                total = one if total is None else total + one
            tok[X, j] = total.astype(BF16)
            return carry

        lax.fori_loop(0, OCT, body, 0)
        copies = [
            pltpu.make_async_copy(
                tok.at[X, j], tg_hbm.at[:, pl.ds(j * oct_w, oct_w)], load_sem.at[0, j]
            )
            for j in range(OCT)
        ]
        for copy in copies:
            copy.start()
        for copy in copies:
            copy.wait()

    build_q(0)
    for copy in loads[:OCT]:
        copy.wait()
    fill(X, 0)
    pl.semaphore_wait(barrier, n_e - 1 + 2)
    dispatch(X, 0)
    for copy in loads[OCT:]:
        copy.wait()
    for j in range(OCT):
        tok[Y, j] = (tok[Y, j].astype(F32) * probs[...]).astype(BF16)
    fill(Y, 0)
    dispatch(Y, 0)
    build_q(1)
    fill(X, 1)
    dispatch(X, 1)
    own(X, 0)
    fill(Y, 1)
    dispatch(Y, 1)
    own(Y, 0)
    build_q(2)
    for a in (X, Y):
        fill(a, 2)
        dispatch(a, 2)
    arrive(X, 0)
    for copy in weights:
        copy.wait()
    own(X, 1)
    arrive(Y, 0)
    complete(X, 0)
    forward(0)
    own(Y, 1)
    arrive(X, 1)
    complete(Y, 0)
    sent(Y, 0)
    backward(0)
    start_reduce(0)
    own(X, 2)
    arrive(Y, 1)
    pass_on(0)
    complete(X, 1)
    forward(1)
    own(Y, 2)
    arrive(X, 2)
    complete(Y, 1)
    sent(Y, 1)
    backward(1)
    start_reduce(1)
    finish(0)
    arrive(Y, 2)
    pass_on(1)
    complete(X, 2)
    forward(2)
    complete(Y, 2)
    sent(Y, 2)
    backward(2)
    start_reduce(2)
    finish(1)
    pass_on(2)
    weight_grads()
    finish(2)
    token_grads()
    for c in range(CHUNKS):
        sent(X, c)
        dispatched(Y, c).wait_send()
        for way in range(2):
            for slot in range(3):
                toward(c, way, slot).wait_send()
        scattered(send.at[X, c], back_of(c), ret_send.at[c], ret_recv.at[c]).wait_send()


def local(tokens, out_grad, expert_ids, route_probs, w_gate, w_up, w_down):
    n_e = lax.axis_size("expert")
    n_x = lax.axis_size("dp")
    toks, width = tokens.shape
    gate_w, up_w, down_w = w_gate[0], w_up[0], w_down[0]
    quarter = gate_w.shape[1]
    oct_w = width // OCT
    chunk_rows = n_x * n_e * PER
    bw = 512 if width % 512 == 0 else 128
    vmem = pl.BlockSpec(memory_space=pltpu.VMEM)
    hbm = pl.BlockSpec(memory_space=pl.ANY)
    dma = pltpu.SemaphoreType.DMA
    token_grad, gate_grad, up_grad = pl.pallas_call(
        kernel,
        out_shape=(
            jax.ShapeDtypeStruct((toks, width), BF16),
            jax.ShapeDtypeStruct((width, quarter), BF16),
            jax.ShapeDtypeStruct((width, quarter), BF16),
        ),
        in_specs=[vmem] * 3 + [hbm] * 5,
        out_specs=(hbm, hbm, hbm),
        scratch_shapes=[
            pltpu.VMEM((2, OCT, toks, oct_w), BF16),
            pltpu.VMEM((n_e * SLAB, OCT * toks), BF16),
            pltpu.VMEM((width, quarter), BF16),
            pltpu.VMEM((width, quarter), BF16),
            pltpu.VMEM((quarter, width), BF16),
            pltpu.VMEM((2, CHUNKS, n_e, SLAB, oct_w), BF16),
            pltpu.VMEM((2, CHUNKS, n_e, SLAB, oct_w), BF16),
            pltpu.VMEM((2, CHUNKS, 2 * n_x, n_e, width), BF16),
            pltpu.VMEM((CHUNKS, 2, n_e, width), BF16),
            pltpu.VMEM((CHUNKS, 2, 2, n_e, width), BF16),
            pltpu.VMEM((n_e, SLAB, oct_w), BF16),
            pltpu.VMEM((3, chunk_rows, quarter), F32),
            pltpu.VMEM((CHUNKS * chunk_rows, 2 * quarter), BF16),
            pltpu.VMEM((2, 2, bw, quarter), BF16),
            dma((3, OCT)),
            dma((2, CHUNKS)),
            dma((2, CHUNKS)),
            dma((2, CHUNKS)),
            dma((2, CHUNKS, 2, 3)),
            dma((2, CHUNKS, 2, 3)),
            dma((CHUNKS, 2, 3)),
            dma((CHUNKS, 2, 3)),
            dma((CHUNKS,)),
            dma((CHUNKS,)),
            dma((CHUNKS,)),
            dma((2, 2)),
        ],
        compiler_params=pltpu.CompilerParams(
            collective_id=0, has_side_effects=True, vmem_limit_bytes=127 * 2**19
        ),
    )(
        expert_ids,
        expert_ids.reshape(1, toks),
        route_probs,
        tokens,
        out_grad,
        gate_w,
        up_w,
        down_w,
    )
    return token_grad, gate_grad[None], up_grad[None]


def solution(mesh):
    in_specs = (
        P(("dp", "expert"), None),
        P(("dp", "expert"), None),
        P(("dp", "expert"), None),
        P(("dp", "expert"), None),
        P("expert", None, "dp"),
        P("expert", None, "dp"),
        P("expert", "dp", None),
    )
    out_specs = (P(("dp", "expert"), None), P("expert", None, "dp"), P("expert", None, "dp"))
    return jax.shard_map(local, mesh=mesh, in_specs=in_specs, out_specs=out_specs, check_vma=False)
```

time: 771 us -> 325 us (0.42)
  waiting for transfers between devices: 528 us -> 0 us
  Pallas kernels: 0 us -> 313 us
  local copies, waits for them, and re-layouts: 111 us -> 11 us
  matrix products: 70.5 us -> 0 us
  starting transfers between devices: 41.9 us -> 0 us
  other arithmetic: 11.2 us -> 0 us
    all_to_all x3 -> x0, waiting for transfers between devices: 528 us -> none  [the longest x1 179 us: local(): lax.all_to_all(pieces_out, ('dp', 'expert'), split_axis=0, concat_axis=0,...]
    pallas_call x0 -> x1, Pallas kernels: none -> 313 us  [local(): pl.pallas_call(kernel, out_shape=(jax.ShapeDtypeStruct((toks, width), BF1...]
    all_to_all x5 -> x0, local copies, waits for them, and re-layouts: 79.9 us -> none  [the longest x2 32.3 us: local(): lax.all_to_all(copies_x, ('dp', 'expert'), split_axis=0, concat_axis=0, t...]
    dot_general x10 -> x0, matrix products: 70.5 us -> none  [the longest x2 18.1 us: contract_rows(): lax.dot_general(x_rows, grads, (((0,), (0,)), ((), ())), preferred_elemen...]
    all_to_all x3 -> x0, starting transfers between devices: 41.9 us -> none  [the longest x1 17.8 us: local(): lax.all_to_all(pieces_out, ('dp', 'expert'), split_axis=0, concat_axis=0,...]
    reshape x1 -> x0, local copies, waits for them, and re-layouts: 16.5 us -> none  [local(): received.reshape(groups, own_rows, model_width).astype(jnp.float32)]
    another operation x2 -> x0, local copies, waits for them, and re-layouts: 14.5 us -> none  [the longest x1 7.32 us: local(): copies_x = jnp.tile(send_x, (groups, 1))]
    unnamed x12 -> x9, local copies, waits for them, and re-layouts: 0.03 us -> 11 us
  transfers between devices with their start and end apart: 3 -> 0, of which waited for: 3 -> 0; matrix products, arithmetic and copies ran while one was open for 5% -> 0% of each run, Pallas kernels for 0% -> 0%
where the time goes in v1:
time: 325 us; the launch traced here: 324 us
  Pallas kernels  313 us (96%)
  local copies, waits for them, and re-layouts  11 us (3%)
    pallas_call x1, Pallas kernels, local(): pl.pallas_call(kernel, out_shape=(jax.ShapeDtypeStruct((toks, width), BF1...  313 us
    unnamed x9, local copies, waits for them, and re-layouts  11 us

profile of v1, /device:TPU:1, one launch (start us, length us, event | category | flops | bytes accessed | tf_op | source)
XLA Modules:
  0.0 324.4 jit_solution(879909703805993357)
XLA Ops:
  0.6 1.4 copy.11.probs
  2.0 1.4 copy.10.ids_col
  3.4 312.8 %shard_map.94 = (bf16[128,7168]{1,0:T(8,128)(2,1)}, bf16[7168,256]{1,0:T(8,128)(2,1)}, bf16[7168,256]{1,0:T(8,128)(2,1)}) custom-call(s32[128,1]{1,0:T(8,128)} %copy.10.ids_col, s32[1,128]{1,0:T(1,128)} %bitcast.11, f32[128,1]{1,0:T(8,128)} %copy.11.probs, bf16[128,7168]{1,0:T(8,128)(2,1)} %tok_hbm.1, bf16[128,7168]{1,0:T(8,128)(2,1)} %og_hbm.1, ...), custom_call_target="tpu_custom_call" | custom-call | tf_op jit(solution)/shard_map/pallas_call | solution.py:447
  316.2 0.0 copy-start.1
  316.2 3.0 copy.15
  319.2 0.0 copy-done.1
  319.2 0.0 copy-start
  319.2 1.9 copy.16
  321.1 1.5 copy-done
  322.6 1.8 copy.17
Async XLA Ops:
  316.2 3.0 copy-start.1
  319.2 3.4 %copy-start = (bf16[7168,256]{1,0:T(8,128)(2,1)S(1)}, bf16[7168,256]{1,0:T(8,128)(2,1)}, u32[]{:S(2)}) copy-start(bf16[7168,256]{1,0:T(8,128)(2,1)} %get-tuple-element.8) | copy-start | bytes 11010052

commit v2 on v1

--- a/solution.py
+++ b/solution.py
@@ -26,11 +26,11 @@
 
 
 def kernel(
-    ids_col, ids_row, probs, tok_hbm, og_hbm, wg_hbm, wu_hbm, wd_hbm,
-    tg_hbm, gg_hbm, ug_hbm,
-    tok, q, wg, wu, wd, send, recv, rows, relay, fin, back, acc, grads, stage,
-    load_sem, disp_send, disp_recv, own_sem, ag_send, ag_recv, rs_send, rs_recv,
-    ret_send, ret_recv, retown_sem, out_sem,
+    ids_ref, probs_ref, tok_hbm, og_hbm, wg_hbm, wu_hbm, wd_hbm,
+    tg_hbm, gg_hbm, ug_hbm, fin_hbm,
+    tok, q, wg, wu, wd, wp, send, recv, rows, relay, fin, back, acc, part_acc, ex_out, ex_in, grads,
+    load_sem, disp_send, disp_recv, own_sem, ag_send, ag_recv, y_send, y_recv, w_send, w_recv,
+    ex_send, ex_recv, rs_send, rs_recv, ret_send, ret_recv, retown_sem, out_sem, fin_sem,
 ):
     n_x = lax.axis_size("dp")
     n_e = lax.axis_size("expert")
@@ -38,6 +38,7 @@
     me_e = lax.axis_index("expert")
     nbr = (lax.rem(me_x + 1, n_x), lax.rem(me_x + n_x - 1, n_x))
     far = lax.rem(me_x + 2, n_x)
+    pair = (me_x + 1 - 2 * lax.rem(me_x, 2), n_x - 1 - me_x)
     toks, width = tok_hbm.shape
     oct_w = width // OCT
     quarter = wg_hbm.shape[1]
@@ -74,12 +75,18 @@
     for x in nbr:
         pl.semaphore_signal(barrier, inc=1, device_id=(x, me_e), device_id_type=MESH)
 
-    same = ids_col[...] == ids_row[...]
     first, second = iota((toks, toks), 0), iota((toks, toks), 1)
+
+    def upright(row):
+        return jnp.sum(jnp.where(first == second, row, jnp.zeros_like(row)), axis=1, keepdims=True)
+
+    ids_row = ids_ref[...]
+    ids_col, probs = upright(ids_row), upright(probs_ref[...])
+    same = ids_col == ids_row
     rank_row = jnp.sum(jnp.where(same & (first < second), 1, 0), axis=0, keepdims=True)
     rank_col = jnp.sum(jnp.where(same & (second < first), 1, 0), axis=1, keepdims=True)
-    key_row = ids_row[...] * PER + (rank_row & 1)
-    key_col = ids_col[...] * PER + (rank_col & 1)
+    key_row = ids_row * PER + (rank_row & 1)
+    key_col = ids_col * PER + (rank_col & 1)
 
     n_slab_rows = n_e * SLAB
     step = min(128, n_slab_rows)
@@ -89,11 +96,11 @@
         i = iota((n_slab_rows, 1), 0)
         for j in range(OCT):
             want = jnp.where(((i >> 1) & (OCT - 1)) == j, (i >> 4) * PER + (i & 1), -2)
-            q[:, j * toks : (j + 1) * toks] = jnp.where(want == keyc, 1.0, 0.0).astype(BF16)
+            q[:n_slab_rows, j * toks : (j + 1) * toks] = jnp.where(want == keyc, 1.0, 0.0).astype(BF16)
 
     def fill(a, c):
         def body(m, carry):
-            part = q[pl.ds(pl.multiple_of(m * step, step), step), :]
+            part = q[pl.ds(pl.multiple_of(m * step, step), step), : OCT * toks]
             out = dot(part, tok[a].reshape(OCT * toks, oct_w)).astype(BF16)
             send[a, c, pl.ds(m * (step // SLAB), step // SLAB)] = out.reshape(
                 step // SLAB, SLAB, oct_w
@@ -142,8 +149,8 @@
         return pltpu.make_async_remote_copy(
             src_ref=ref,
             dst_ref=ref,
-            send_sem=ag_send.at[a, c, way, slot],
-            recv_sem=ag_recv.at[a, c, way, slot],
+            send_sem=ag_send.at[c, way, slot],
+            recv_sem=ag_recv.at[c, way, slot],
             device_id=(nbr[way], me_e),
             device_id_type=MESH,
         )
@@ -154,7 +161,7 @@
         j, rest = row >> log_half, row & (half - 1)
         return jnp.where(col == (rest >> 1) * SLAB + j * PER + (rest & 1), 1.0, 0.0).astype(BF16)
 
-    def own(a, c):
+    def collect(a, c):
         pltpu.make_async_copy(send.at[a, c, me_e], recv.at[a, c, me_e], own_sem.at[a, c]).wait()
         dispatched(a, c).wait_recv()
         order = perm(iota((size, size), 0), iota((size, size), 1))
@@ -165,27 +172,68 @@
                 rows[a, c, me_x * 2 + h, :, j * oct_w : (j + 1) * oct_w] = out[
                     j * half : (j + 1) * half
                 ]
-        hop(a, c, me_x, 0, 0, 0).start()
-        hop(a, c, me_x, 1, 1, 1).start()
-        hop(a, c, me_x, 1, 0, 1).start()
-        hop(a, c, me_x, 0, 1, 0).start()
-
-    def arrive(a, c):
+
+    def own(c):
+        collect(X, c)
+        hop(X, c, me_x, 0, 0, 0).start()
+        hop(X, c, me_x, 1, 1, 1).start()
+        hop(X, c, me_x, 1, 0, 1).start()
+        hop(X, c, me_x, 0, 1, 0).start()
+
+    wide = width // 2
+
+    def swap_weight(i):
+        return pltpu.make_async_remote_copy(
+            src_ref=wd_hbm.at[:, pl.ds(i * wide, wide)],
+            dst_ref=wp.at[i],
+            send_sem=w_send.at[i],
+            recv_sem=w_recv.at[i],
+            device_id=(pair[i], me_e),
+            device_id_type=MESH,
+        )
+
+    def lend(c, i, block):
+        ref = rows.at[Y, c, pl.ds(block * 2, 2), :, pl.ds(i * wide, wide)]
+        return pltpu.make_async_remote_copy(
+            src_ref=ref,
+            dst_ref=ref,
+            send_sem=y_send.at[c, i],
+            recv_sem=y_recv.at[c, i],
+            device_id=(pair[1 - i], me_e),
+            device_id_type=MESH,
+        )
+
+    def own_y(c):
+        collect(Y, c)
+        for i in range(2):
+            lend(c, i, me_x).start()
+
+    def exchange(c, i):
+        return pltpu.make_async_remote_copy(
+            src_ref=ex_out.at[c, i],
+            dst_ref=ex_in.at[c, i],
+            send_sem=ex_send.at[c, i],
+            recv_sem=ex_recv.at[c, i],
+            device_id=(pair[i], me_e),
+            device_id_type=MESH,
+        )
+
+    def arrive(c):
         for way in range(2):
             block = nbr[1 - way]
-            hop(a, c, block, way, way, way).wait_recv()
-            hop(a, c, block, way, way, 2).start()
-
-    def complete(a, c):
+            hop(X, c, block, way, way, way).wait_recv()
+            hop(X, c, block, way, way, 2).start()
+
+    def complete(c):
         for way in range(2):
-            hop(a, c, nbr[1 - way], 1 - way, way, 1 - way).wait_recv()
-            hop(a, c, far, way, way, 2).wait_recv()
-
-    def sent(a, c):
+            hop(X, c, nbr[1 - way], 1 - way, way, 1 - way).wait_recv()
+            hop(X, c, far, way, way, 2).wait_recv()
+
+    def sent(c):
         for way in range(2):
             for slot in range(2):
-                hop(a, c, me_x, slot, way, slot).wait_send()
-            hop(a, c, nbr[1 - way], way, way, 2).wait_send()
+                hop(X, c, me_x, slot, way, slot).wait_send()
+            hop(X, c, nbr[1 - way], way, way, 2).wait_send()
 
     kw = width // 4
 
@@ -193,8 +241,8 @@
         def body(k, carry):
             cols = pl.ds(pl.multiple_of(k * kw, 128), kw)
             x = rows[X, c, :, :, cols].reshape(chunk_rows, kw)
-            g = dot(x, wg[cols, :])
-            u = dot(x, wu[cols, :])
+            g = dot(x, wg[cols, :]).reshape(acc.shape[1:])
+            u = dot(x, wu[cols, :]).reshape(acc.shape[1:])
 
             @pl.when(k == 0)
             def _():
@@ -212,24 +260,57 @@
 
     bw = 512 if width % 512 == 0 else 128
 
+    block_rows = 2 * half
+
+    def partial(c):
+        for i in range(2):
+            lend(c, i, pair[1 - i]).wait_recv()
+            if c == 0:
+                swap_weight(i).wait_recv()
+
+            def body(k, carry):
+                step_w = wide // 4
+                near = pl.ds(pl.multiple_of(k * step_w, 128), step_w)
+                cols = pl.ds(pl.multiple_of(i * wide + k * step_w, 128), step_w)
+                y = jnp.concatenate(
+                    [
+                        rows[Y, c, pl.ds(p * 2, 2), :, cols].reshape(block_rows, step_w)
+                        for p in (me_x, pair[1 - i])
+                    ],
+                    axis=0,
+                )
+                mine = dot(y, wd[:, cols], NT)
+                lent = dot(y, wp[i, :, near], NT)
+
+                @pl.when(k == 0)
+                def _():
+                    part_acc[0] = mine
+                    part_acc[1] = lent
+
+                @pl.when(k > 0)
+                def _():
+                    part_acc[0] += mine
+                    part_acc[1] += lent
+
+                return carry
+
+            lax.fori_loop(0, 4, body, 0)
+            ex_out[c, i] = part_acc[1].astype(BF16)
+            exchange(c, i).start()
+            if i == 0:
+                acc[2, me_x] = part_acc[0, :block_rows]
+            else:
+                acc[2, me_x] += part_acc[0, :block_rows]
+            acc[2, pair[1 - i]] = part_acc[0, block_rows:]
+
     def backward(c):
-        def body(k, carry):
-            cols = pl.ds(pl.multiple_of(k * kw, 128), kw)
-            y = rows[Y, c, :, :, cols].reshape(chunk_rows, kw)
-            h = dot(y, wd[:, cols], NT)
-
-            @pl.when(k == 0)
-            def _():
-                acc[2] = h
-
-            @pl.when(k > 0)
-            def _():
-                acc[2] += h
-
-            return carry
-
-        lax.fori_loop(0, 4, body, 0)
-        gate_val, up_val, hidden = acc[0], acc[1], acc[2]
+        for i in range(2):
+            exchange(c, i).wait_recv()
+            lend(c, i, me_x).wait_send()
+        for i in range(2):
+            acc[2, pair[i]] += ex_in[c, i, :block_rows].astype(F32)
+        acc[2, far] = ex_in[c, 0, block_rows:].astype(F32) + ex_in[c, 1, block_rows:].astype(F32)
+        gate_val, up_val, hidden = (acc[n].reshape(chunk_rows, quarter) for n in range(3))
         s = jax.nn.sigmoid(gate_val)
         grad_up = (hidden * gate_val * s).astype(BF16)
         grad_gate = (hidden * up_val * s * (1.0 + gate_val * (1.0 - s))).astype(BF16)
@@ -249,11 +330,14 @@
     def back_of(c):
         return (recv.at[X, 0], recv.at[Y, 0], back)[c]
 
+    def last_of(c):
+        return fin if c == CHUNKS - 1 else fin_hbm.at[c]
+
     def toward(c, way, slot):
         dst_block = far if slot == 0 else nbr[way]
         h = (way, 1 - way, way)[slot]
         src = rows.at[Y, c, dst_block * 2 + h]
-        dst = relay.at[c, way] if slot == 0 else fin.at[c, way, h]
+        dst = relay.at[c, way] if slot == 0 else last_of(c).at[way, h]
         return pltpu.make_async_remote_copy(
             src_ref=src,
             dst_ref=dst,
@@ -289,24 +373,37 @@
             for slot in (1, 2):
                 toward(c, way, slot).wait_recv()
         for h in range(2):
+            if c < CHUNKS - 1:
+                fetch = [
+                    pltpu.make_async_copy(fin_hbm.at[c, way, h], relay.at[c, way], fin_sem.at[way])
+                    for way in range(2)
+                ]
+                for copy in fetch:
+                    copy.start()
+                for copy in fetch:
+                    copy.wait()
+            came = (relay.at[c, 0], relay.at[c, 1]) if c < CHUNKS - 1 else (fin.at[0, h], fin.at[1, h])
             blocks = []
             for j in range(OCT):
                 cols = slice(j * oct_w, (j + 1) * oct_w)
                 total = (
                     rows[Y, c, me_x * 2 + h, :, cols].astype(F32)
-                    + fin[c, 0, h, :, cols].astype(F32)
-                    + fin[c, 1, h, :, cols].astype(F32)
+                    + came[0][:, cols].astype(F32)
+                    + came[1][:, cols].astype(F32)
                 )
                 blocks.append(total.astype(BF16))
             out = dot(order, jnp.concatenate(blocks, axis=0)).astype(BF16)
             send[X, c, h * gs : (h + 1) * gs] = out.reshape(gs, SLAB, oct_w)
         scatter(send.at[X, c], back_of(c), ret_send.at[c], ret_recv.at[c], retown_sem.at[c])
 
+    def stage(slot, o):
+        return q.at[pl.ds(0, bw), pl.ds(pl.multiple_of((slot * 2 + o) * quarter, 128), quarter)]
+
     def weight_grads():
         def tile(i, slot):
             cols = pl.ds(pl.multiple_of(i * bw, 128), bw)
             return [
-                pltpu.make_async_copy(stage.at[slot, o], dst.at[cols, :], out_sem.at[slot, o])
+                pltpu.make_async_copy(stage(slot, o), dst.at[cols, :], out_sem.at[slot, o])
                 for o, dst in ((0, gg_hbm), (1, ug_hbm))
             ]
 
@@ -321,8 +418,8 @@
             cols = pl.ds(pl.multiple_of(i * bw, 128), bw)
             x = rows[X, :, :, :, cols].reshape(CHUNKS * chunk_rows, bw)
             out = dot(x, grads[...], TN).astype(BF16)
-            stage[slot, 0] = out[:, :quarter]
-            stage[slot, 1] = out[:, quarter:]
+            stage(slot, 0)[...] = out[:, :quarter]
+            stage(slot, 1)[...] = out[:, quarter:]
             for copy in tile(i, slot):
                 copy.start()
             return carry
@@ -363,59 +460,55 @@
             copy.wait()
 
     build_q(0)
+    pl.semaphore_wait(barrier, n_e - 1 + 2)
+    for i in range(2):
+        swap_weight(i).start()
     for copy in loads[:OCT]:
         copy.wait()
     fill(X, 0)
-    pl.semaphore_wait(barrier, n_e - 1 + 2)
     dispatch(X, 0)
     for copy in loads[OCT:]:
         copy.wait()
     for j in range(OCT):
-        tok[Y, j] = (tok[Y, j].astype(F32) * probs[...]).astype(BF16)
+        tok[Y, j] = (tok[Y, j].astype(F32) * probs).astype(BF16)
     fill(Y, 0)
     dispatch(Y, 0)
     build_q(1)
     fill(X, 1)
     dispatch(X, 1)
-    own(X, 0)
+    own(0)
     fill(Y, 1)
     dispatch(Y, 1)
-    own(Y, 0)
+    own_y(0)
     build_q(2)
     for a in (X, Y):
         fill(a, 2)
         dispatch(a, 2)
-    arrive(X, 0)
+    arrive(0)
     for copy in weights:
         copy.wait()
-    own(X, 1)
-    arrive(Y, 0)
-    complete(X, 0)
+    own(1)
+    own_y(1)
+    complete(0)
     forward(0)
-    own(Y, 1)
-    arrive(X, 1)
-    complete(Y, 0)
-    sent(Y, 0)
+    partial(0)
+    arrive(1)
+    own(2)
+    own_y(2)
     backward(0)
     start_reduce(0)
-    own(X, 2)
-    arrive(Y, 1)
+    complete(1)
+    forward(1)
+    partial(1)
+    arrive(2)
     pass_on(0)
-    complete(X, 1)
-    forward(1)
-    own(Y, 2)
-    arrive(X, 2)
-    complete(Y, 1)
-    sent(Y, 1)
     backward(1)
     start_reduce(1)
     finish(0)
-    arrive(Y, 2)
+    complete(2)
+    forward(2)
+    partial(2)
     pass_on(1)
-    complete(X, 2)
-    forward(2)
-    complete(Y, 2)
-    sent(Y, 2)
     backward(2)
     start_reduce(2)
     finish(1)
@@ -424,12 +517,16 @@
     finish(2)
     token_grads()
     for c in range(CHUNKS):
-        sent(X, c)
+        sent(c)
         dispatched(Y, c).wait_send()
+        for i in range(2):
+            exchange(c, i).wait_send()
         for way in range(2):
             for slot in range(3):
                 toward(c, way, slot).wait_send()
         scattered(send.at[X, c], back_of(c), ret_send.at[c], ret_recv.at[c]).wait_send()
+    for i in range(2):
+        swap_weight(i).wait_send()
 
 
 def local(tokens, out_grad, expert_ids, route_probs, w_gate, w_up, w_down):
@@ -444,50 +541,60 @@
     vmem = pl.BlockSpec(memory_space=pltpu.VMEM)
     hbm = pl.BlockSpec(memory_space=pl.ANY)
     dma = pltpu.SemaphoreType.DMA
-    token_grad, gate_grad, up_grad = pl.pallas_call(
+    token_grad, gate_grad, up_grad, _ = pl.pallas_call(
         kernel,
         out_shape=(
             jax.ShapeDtypeStruct((toks, width), BF16),
             jax.ShapeDtypeStruct((width, quarter), BF16),
             jax.ShapeDtypeStruct((width, quarter), BF16),
+            jax.ShapeDtypeStruct((CHUNKS - 1, 2, 2, n_e, width), BF16),
         ),
-        in_specs=[vmem] * 3 + [hbm] * 5,
-        out_specs=(hbm, hbm, hbm),
+        in_specs=[vmem] * 2 + [hbm] * 5,
+        out_specs=(hbm, hbm, hbm, hbm),
         scratch_shapes=[
             pltpu.VMEM((2, OCT, toks, oct_w), BF16),
-            pltpu.VMEM((n_e * SLAB, OCT * toks), BF16),
+            pltpu.VMEM((max(n_e * SLAB, bw), max(OCT * toks, 4 * quarter)), BF16),
             pltpu.VMEM((width, quarter), BF16),
             pltpu.VMEM((width, quarter), BF16),
             pltpu.VMEM((quarter, width), BF16),
+            pltpu.VMEM((2, quarter, width // 2), BF16),
             pltpu.VMEM((2, CHUNKS, n_e, SLAB, oct_w), BF16),
             pltpu.VMEM((2, CHUNKS, n_e, SLAB, oct_w), BF16),
             pltpu.VMEM((2, CHUNKS, 2 * n_x, n_e, width), BF16),
             pltpu.VMEM((CHUNKS, 2, n_e, width), BF16),
-            pltpu.VMEM((CHUNKS, 2, 2, n_e, width), BF16),
+            pltpu.VMEM((2, 2, n_e, width), BF16),
             pltpu.VMEM((n_e, SLAB, oct_w), BF16),
-            pltpu.VMEM((3, chunk_rows, quarter), F32),
+            pltpu.VMEM((3, n_x, n_e * PER, quarter), F32),
+            pltpu.VMEM((2, 2 * n_e * PER, quarter), F32),
+            pltpu.VMEM((CHUNKS, 2, 2 * n_e * PER, quarter), BF16),
+            pltpu.VMEM((CHUNKS, 2, 2 * n_e * PER, quarter), BF16),
             pltpu.VMEM((CHUNKS * chunk_rows, 2 * quarter), BF16),
-            pltpu.VMEM((2, 2, bw, quarter), BF16),
             dma((3, OCT)),
             dma((2, CHUNKS)),
             dma((2, CHUNKS)),
             dma((2, CHUNKS)),
-            dma((2, CHUNKS, 2, 3)),
-            dma((2, CHUNKS, 2, 3)),
+            dma((CHUNKS, 2, 3)),
+            dma((CHUNKS, 2, 3)),
+            dma((CHUNKS, 2)),
+            dma((CHUNKS, 2)),
+            dma((2,)),
+            dma((2,)),
+            dma((CHUNKS, 2)),
+            dma((CHUNKS, 2)),
             dma((CHUNKS, 2, 3)),
             dma((CHUNKS, 2, 3)),
             dma((CHUNKS,)),
             dma((CHUNKS,)),
             dma((CHUNKS,)),
             dma((2, 2)),
+            dma((2,)),
         ],
         compiler_params=pltpu.CompilerParams(
             collective_id=0, has_side_effects=True, vmem_limit_bytes=127 * 2**19
         ),
     )(
-        expert_ids,
         expert_ids.reshape(1, toks),
-        route_probs,
+        route_probs.reshape(1, toks),
         tokens,
         out_grad,
         gate_w,

time: 325 us -> 292 us (0.90)
  Pallas kernels: 313 us -> 282 us
    pallas_call x1, Pallas kernels: 313 us -> 282 us  [local(): pl.pallas_call(kernel, out_shape=(jax.ShapeDtypeStruct((toks, width), BF1...]
    unnamed x9 -> x7, local copies, waits for them, and re-layouts: 11 us -> 8.2 us
where the time goes in v2:
time: 292 us; the launch traced here: 291 us
  Pallas kernels  282 us (97%)
  local copies, waits for them, and re-layouts  8.2 us (3%)
    pallas_call x1, Pallas kernels, local(): pl.pallas_call(kernel, out_shape=(jax.ShapeDtypeStruct((toks, width), BF1...  282 us
    unnamed x7, local copies, waits for them, and re-layouts  8.2 us

profile of v2, /device:TPU:1, one launch (start us, length us, event | category | flops | bytes accessed | tf_op | source)
XLA Modules:
  0.0 291.3 jit_solution(5483689688677132260)
XLA Ops:
  0.6 282.5 %shard_map.94 = (bf16[128,7168]{1,0:T(8,128)(2,1)}, bf16[7168,256]{1,0:T(8,128)(2,1)}, bf16[7168,256]{1,0:T(8,128)(2,1)}, bf16[2,2,2,32,7168]{4,3,2,1,0:T(8,128)(2,1)}) custom-call(s32[1,128]{1,0:T(1,128)} %bitcast.12, f32[1,128]{1,0:T(1,128)} %bitcast.13, bf16[128,7168]{1,0:T(8,128)(2,1)} %tok_hbm.1, bf16[128,7168]{1,0:T(8,128)(2,1)} %og_hbm.1, ...), custom_call_target="tpu_custom_call" | custom-call | tf_op jit(solution)/shard_map/pallas_call | solution.py:544
  283.1 0.0 copy-start.1
  283.1 3.0 %copy.13 = bf16[128,7168]{1,0:T(8,128)(2,1)} copy(bf16[128,7168]{1,0:T(8,128)(2,1)} %get-tuple-element.12) | data formatting | bytes 3670016
  286.1 0.0 copy-done.1
  286.1 0.0 copy-start
  286.1 1.9 copy.14
  288.0 1.5 copy-done
  289.5 1.8 copy.15
Async XLA Ops:
  283.1 3.0 %copy-start.1 = (bf16[7168,256]{1,0:T(8,128)(2,1)S(1)}, bf16[7168,256]{1,0:T(8,128)(2,1)}, u32[]{:S(2)}) copy-start(bf16[7168,256]{1,0:T(8,128)(2,1)} %get-tuple-element.7) | copy-start | bytes 11010052
  286.1 3.4 %copy-start = (bf16[7168,256]{1,0:T(8,128)(2,1)S(1)}, bf16[7168,256]{1,0:T(8,128)(2,1)}, u32[]{:S(2)}) copy-start(bf16[7168,256]{1,0:T(8,128)(2,1)} %get-tuple-element.8) | copy-start | bytes 11010052

commit v3 on v2

--- a/solution.py
+++ b/solution.py
@@ -25,10 +25,29 @@
     return lax.broadcasted_iota(jnp.int32, shape, axis)
 
 
+def slot_keys(ids_row):
+    toks = ids_row.shape[1]
+    first, second = iota((toks, toks), 0), iota((toks, toks), 1)
+    ids_col = upright(ids_row)
+    same = ids_col == ids_row
+    rank_row = jnp.sum(jnp.where(same & (first < second), 1, 0), axis=0, keepdims=True)
+    rank_col = jnp.sum(jnp.where(same & (second < first), 1, 0), axis=1, keepdims=True)
+    return (
+        (rank_row, ids_row * PER + (rank_row & 1)),
+        (rank_col, ids_col * PER + (rank_col & 1)),
+    )
+
+
+def upright(row):
+    toks = row.shape[1]
+    eye = iota((toks, toks), 0) == iota((toks, toks), 1)
+    return jnp.sum(jnp.where(eye, row, jnp.zeros_like(row)), axis=1, keepdims=True)
+
+
 def kernel(
     ids_ref, probs_ref, tok_hbm, og_hbm, wg_hbm, wu_hbm, wd_hbm,
-    tg_hbm, gg_hbm, ug_hbm, fin_hbm,
-    tok, q, wg, wu, wd, wp, send, recv, rows, relay, fin, back, acc, part_acc, ex_out, ex_in, grads,
+    back, gg_hbm, ug_hbm, fin_hbm,
+    tok, q, wg, wu, wd, wp, send, recv, rows, relay, fin, acc, part_acc, ex_out, ex_in, grads,
     load_sem, disp_send, disp_recv, own_sem, ag_send, ag_recv, y_send, y_recv, w_send, w_recv,
     ex_send, ex_recv, rs_send, rs_recv, ret_send, ret_recv, retown_sem, out_sem, fin_sem,
 ):
@@ -75,18 +94,8 @@
     for x in nbr:
         pl.semaphore_signal(barrier, inc=1, device_id=(x, me_e), device_id_type=MESH)
 
-    first, second = iota((toks, toks), 0), iota((toks, toks), 1)
-
-    def upright(row):
-        return jnp.sum(jnp.where(first == second, row, jnp.zeros_like(row)), axis=1, keepdims=True)
-
-    ids_row = ids_ref[...]
-    ids_col, probs = upright(ids_row), upright(probs_ref[...])
-    same = ids_col == ids_row
-    rank_row = jnp.sum(jnp.where(same & (first < second), 1, 0), axis=0, keepdims=True)
-    rank_col = jnp.sum(jnp.where(same & (second < first), 1, 0), axis=1, keepdims=True)
-    key_row = ids_row * PER + (rank_row & 1)
-    key_col = ids_col * PER + (rank_col & 1)
+    (rank_row, key_row), _ = slot_keys(ids_ref[...])
+    probs = upright(probs_ref[...])
 
     n_slab_rows = n_e * SLAB
     step = min(128, n_slab_rows)
@@ -156,9 +165,17 @@
         )
 
     size = gs * SLAB
+    piece = half // 2
+    piece_size = size // 2
 
     def perm(row, col):
         j, rest = row >> log_half, row & (half - 1)
+        at = rest >> 1
+        slab = (at & (gs // 2 - 1)) * 2 + (at >> (log_half - 2))
+        return jnp.where(col == slab * SLAB + j * PER + (rest & 1), 1.0, 0.0).astype(BF16)
+
+    def piece_perm(row, col):
+        j, rest = row >> (log_half - 1), row & (piece - 1)
         return jnp.where(col == (rest >> 1) * SLAB + j * PER + (rest & 1), 1.0, 0.0).astype(BF16)
 
     def collect(a, c):
@@ -327,74 +344,106 @@
 
         lax.fori_loop(0, width // bw, part, 0)
 
-    def back_of(c):
-        return (recv.at[X, 0], recv.at[Y, 0], back)[c]
-
     def last_of(c):
         return fin if c == CHUNKS - 1 else fin_hbm.at[c]
 
-    def toward(c, way, slot):
+    def toward(c, p, way, slot):
         dst_block = far if slot == 0 else nbr[way]
         h = (way, 1 - way, way)[slot]
-        src = rows.at[Y, c, dst_block * 2 + h]
-        dst = relay.at[c, way] if slot == 0 else last_of(c).at[way, h]
+        part = pl.ds(p * piece, piece)
+        src = rows.at[Y, c, dst_block * 2 + h, part]
+        dst = relay.at[c, way, part] if slot == 0 else last_of(c).at[way, h, part]
         return pltpu.make_async_remote_copy(
             src_ref=src,
             dst_ref=dst,
-            send_sem=rs_send.at[c, way, slot],
-            recv_sem=rs_recv.at[c, way, slot],
+            send_sem=rs_send.at[c, p, way, slot],
+            recv_sem=rs_recv.at[c, p, way, slot],
             device_id=(nbr[way], me_e),
             device_id_type=MESH,
         )
 
     def start_reduce(c):
-        for slot in range(2):
+        for p in range(2):
+            for slot in range(2):
+                for way in range(2):
+                    toward(c, p, way, slot).start()
+
+    def pass_on(c):
+        for p in range(2):
             for way in range(2):
-                toward(c, way, slot).start()
-
-    def pass_on(c):
-        for way in range(2):
-            toward(c, way, 0).wait_recv()
-
-            def body(d, carry):
-                cols = pl.ds(pl.multiple_of(d * bw, 128), bw)
-                at = nbr[way] * 2 + way
-                total = rows[Y, c, at, :, cols].astype(F32) + relay[c, way, :, cols].astype(F32)
-                rows[Y, c, at, :, cols] = total.astype(BF16)
-                return carry
-
-            lax.fori_loop(0, width // bw, body, 0)
-            toward(c, way, 2).start()
+                toward(c, p, way, 0).wait_recv()
+
+                def body(d, carry):
+                    part = pl.ds(p * piece, piece)
+                    cols = pl.ds(pl.multiple_of(d * bw, 128), bw)
+                    at = nbr[way] * 2 + way
+                    mine = rows[Y, c, at, part, cols].astype(F32)
+                    total = mine + relay[c, way, part, cols].astype(F32)
+                    rows[Y, c, at, part, cols] = total.astype(BF16)
+                    return carry
+
+                lax.fori_loop(0, width // bw, body, 0)
+                toward(c, p, way, 2).start()
+
+    def give_back(c, peer):
+        pltpu.make_async_remote_copy(
+            src_ref=send.at[X, c, peer],
+            dst_ref=back.at[c, me_e],
+            send_sem=ret_send.at[c],
+            recv_sem=ret_recv.at[c],
+            device_id=(me_x, peer),
+            device_id_type=MESH,
+        ).start()
 
     def finish(c):
         dispatched(X, c).wait_send()
-        order = perm(iota((size, size), 1), iota((size, size), 0))
-        for way in range(2):
-            for slot in (1, 2):
-                toward(c, way, slot).wait_recv()
-        for h in range(2):
-            if c < CHUNKS - 1:
-                fetch = [
-                    pltpu.make_async_copy(fin_hbm.at[c, way, h], relay.at[c, way], fin_sem.at[way])
-                    for way in range(2)
-                ]
-                for copy in fetch:
-                    copy.start()
-                for copy in fetch:
-                    copy.wait()
-            came = (relay.at[c, 0], relay.at[c, 1]) if c < CHUNKS - 1 else (fin.at[0, h], fin.at[1, h])
-            blocks = []
-            for j in range(OCT):
-                cols = slice(j * oct_w, (j + 1) * oct_w)
-                total = (
-                    rows[Y, c, me_x * 2 + h, :, cols].astype(F32)
-                    + came[0][:, cols].astype(F32)
-                    + came[1][:, cols].astype(F32)
-                )
-                blocks.append(total.astype(BF16))
-            out = dot(order, jnp.concatenate(blocks, axis=0)).astype(BF16)
-            send[X, c, h * gs : (h + 1) * gs] = out.reshape(gs, SLAB, oct_w)
-        scatter(send.at[X, c], back_of(c), ret_send.at[c], ret_recv.at[c], retown_sem.at[c])
+        order = piece_perm(iota((piece_size, piece_size), 1), iota((piece_size, piece_size), 0))
+        for p in range(2):
+            part = slice(p * piece, (p + 1) * piece)
+            for way in range(2):
+                for slot in (1, 2):
+                    toward(c, p, way, slot).wait_recv()
+            for h in range(2):
+                if c < CHUNKS - 1:
+                    fetch = [
+                        pltpu.make_async_copy(
+                            fin_hbm.at[c, way, h, pl.ds(p * piece, piece)],
+                            relay.at[c, way, pl.ds(p * piece, piece)],
+                            fin_sem.at[way],
+                        )
+                        for way in range(2)
+                    ]
+                    for copy in fetch:
+                        copy.start()
+                    for copy in fetch:
+                        copy.wait()
+                    came = (relay.at[c, 0], relay.at[c, 1])
+                else:
+                    came = (fin.at[0, h], fin.at[1, h])
+                blocks = []
+                for j in range(OCT):
+                    cols = slice(j * oct_w, (j + 1) * oct_w)
+                    total = (
+                        rows[Y, c, me_x * 2 + h, part, cols].astype(F32)
+                        + came[0][part, cols].astype(F32)
+                        + came[1][part, cols].astype(F32)
+                    )
+                    blocks.append(total.astype(BF16))
+                out = dot(order, jnp.concatenate(blocks, axis=0)).astype(BF16)
+                for i in range(gs // 2):
+                    send[X, c, h * gs + 2 * i + p] = out[i * SLAB : (i + 1) * SLAB]
+
+            def body(d, carry):
+                give_back(c, lax.rem(me_e // 2 + d, n_e // 2) * 2 + p)
+                return carry
+
+            lax.fori_loop(1, n_e // 2, body, 0)
+
+            @pl.when(lax.rem(me_e, 2) != p)
+            def _():
+                give_back(c, (me_e // 2) * 2 + p)
+
+        pltpu.make_async_copy(send.at[X, c, me_e], back.at[c, me_e], retown_sem.at[c]).start()
 
     def stage(slot, o):
         return q.at[pl.ds(0, bw), pl.ds(pl.multiple_of((slot * 2 + o) * quarter, 128), quarter)]
@@ -429,35 +478,6 @@
         for i in (n - 2, n - 1):
             for copy in tile(i, i % 2):
                 copy.wait()
-
-    def token_grads():
-        for c in range(CHUNKS):
-            pltpu.make_async_copy(send.at[X, c, me_e], back_of(c).at[me_e], retown_sem.at[c]).wait()
-            scattered(send.at[X, c], back_of(c), ret_send.at[c], ret_recv.at[c]).wait_recv()
-        i = iota((1, n_slab_rows), 1)
-
-        def body(j, carry):
-            want = jnp.where(((i >> 1) & (OCT - 1)) == j, (i >> 4) * PER + (i & 1), -2)
-            total = None
-            for c in range(CHUNKS):
-                keyc = jnp.where((rank_col >> 1) == c, key_col, -1)
-                place = jnp.where(keyc == want, 1.0, 0.0).astype(BF16)
-                one = dot(place, back_of(c)[...].reshape(n_slab_rows, oct_w))
-                total = one if total is None else total + one
-            tok[X, j] = total.astype(BF16)
-            return carry
-
-        lax.fori_loop(0, OCT, body, 0)
-        copies = [
-            pltpu.make_async_copy(
-                tok.at[X, j], tg_hbm.at[:, pl.ds(j * oct_w, oct_w)], load_sem.at[0, j]
-            )
-            for j in range(OCT)
-        ]
-        for copy in copies:
-            copy.start()
-        for copy in copies:
-            copy.wait()
 
     build_q(0)
     pl.semaphore_wait(barrier, n_e - 1 + 2)
@@ -515,18 +535,57 @@
     pass_on(2)
     weight_grads()
     finish(2)
-    token_grads()
     for c in range(CHUNKS):
         sent(c)
         dispatched(Y, c).wait_send()
         for i in range(2):
             exchange(c, i).wait_send()
-        for way in range(2):
-            for slot in range(3):
-                toward(c, way, slot).wait_send()
-        scattered(send.at[X, c], back_of(c), ret_send.at[c], ret_recv.at[c]).wait_send()
+        for p in range(2):
+            for way in range(2):
+                for slot in range(3):
+                    toward(c, p, way, slot).wait_send()
+        pltpu.make_async_copy(send.at[X, c, me_e], back.at[c, me_e], retown_sem.at[c]).wait()
+        scattered(send.at[X, c], back.at[c], ret_send.at[c], ret_recv.at[c]).wait()
     for i in range(2):
         swap_weight(i).wait_send()
+
+
+def place(ids_ref, back_hbm, gg_src, ug_src, tg_hbm, gg_hbm, ug_hbm, back, out, back_sem, tg_sem, grad_sem):
+    width = gg_src.shape[0]
+    n_e = back.shape[1]
+    oct_w = back.shape[3]
+    n_cut = grad_sem.shape[1]
+    cut = width // n_cut
+    came = [pltpu.make_async_copy(back_hbm.at[c], back.at[c], back_sem.at[c]) for c in range(CHUNKS)]
+    moves = [
+        pltpu.make_async_copy(
+            src.at[pl.ds(i * cut, cut)], dst.at[pl.ds(i * cut, cut)], grad_sem.at[o, i]
+        )
+        for i in range(n_cut)
+        for o, (src, dst) in enumerate(((gg_src, gg_hbm), (ug_src, ug_hbm)))
+    ]
+    for copy in came + moves:
+        copy.start()
+    _, (rank_col, key_col) = slot_keys(ids_ref[...])
+    i = iota((1, n_e * SLAB), 1)
+    for copy in came:
+        copy.wait()
+    outs = []
+    for j in range(OCT):
+        want = jnp.where(((i >> 1) & (OCT - 1)) == j, (i >> 4) * PER + (i & 1), -2)
+        total = None
+        for c in range(CHUNKS):
+            keyc = jnp.where((rank_col >> 1) == c, key_col, -1)
+            here = jnp.where(keyc == want, 1.0, 0.0).astype(BF16)
+            one = dot(here, back[c].reshape(n_e * SLAB, oct_w))
+            total = one if total is None else total + one
+        out[j] = total.astype(BF16)
+        outs.append(
+            pltpu.make_async_copy(out.at[j], tg_hbm.at[:, pl.ds(j * oct_w, oct_w)], tg_sem.at[j])
+        )
+        outs[-1].start()
+    for copy in outs + moves:
+        copy.wait()
 
 
 def local(tokens, out_grad, expert_ids, route_probs, w_gate, w_up, w_down):
@@ -541,10 +600,11 @@
     vmem = pl.BlockSpec(memory_space=pltpu.VMEM)
     hbm = pl.BlockSpec(memory_space=pl.ANY)
     dma = pltpu.SemaphoreType.DMA
-    token_grad, gate_grad, up_grad, _ = pl.pallas_call(
+    ids_row = expert_ids.reshape(1, toks)
+    back, gate_grad, up_grad, _ = pl.pallas_call(
         kernel,
         out_shape=(
-            jax.ShapeDtypeStruct((toks, width), BF16),
+            jax.ShapeDtypeStruct((CHUNKS, n_e, SLAB, oct_w), BF16),
             jax.ShapeDtypeStruct((width, quarter), BF16),
             jax.ShapeDtypeStruct((width, quarter), BF16),
             jax.ShapeDtypeStruct((CHUNKS - 1, 2, 2, n_e, width), BF16),
@@ -563,7 +623,6 @@
             pltpu.VMEM((2, CHUNKS, 2 * n_x, n_e, width), BF16),
             pltpu.VMEM((CHUNKS, 2, n_e, width), BF16),
             pltpu.VMEM((2, 2, n_e, width), BF16),
-            pltpu.VMEM((n_e, SLAB, oct_w), BF16),
             pltpu.VMEM((3, n_x, n_e * PER, quarter), F32),
             pltpu.VMEM((2, 2 * n_e * PER, quarter), F32),
             pltpu.VMEM((CHUNKS, 2, 2 * n_e * PER, quarter), BF16),
@@ -581,8 +640,8 @@
             dma((2,)),
             dma((CHUNKS, 2)),
             dma((CHUNKS, 2)),
-            dma((CHUNKS, 2, 3)),
-            dma((CHUNKS, 2, 3)),
+            dma((CHUNKS, 2, 2, 3)),
+            dma((CHUNKS, 2, 2, 3)),
             dma((CHUNKS,)),
             dma((CHUNKS,)),
             dma((CHUNKS,)),
@@ -593,7 +652,7 @@
             collective_id=0, has_side_effects=True, vmem_limit_bytes=127 * 2**19
         ),
     )(
-        expert_ids.reshape(1, toks),
+        ids_row,
         route_probs.reshape(1, toks),
         tokens,
         out_grad,
@@ -601,6 +660,25 @@
         up_w,
         down_w,
     )
+    n_cut = 4
+    token_grad, gate_grad, up_grad = pl.pallas_call(
+        place,
+        out_shape=(
+            jax.ShapeDtypeStruct((toks, width), BF16),
+            jax.ShapeDtypeStruct((width, quarter), BF16),
+            jax.ShapeDtypeStruct((width, quarter), BF16),
+        ),
+        in_specs=[vmem] + [hbm] * 3,
+        out_specs=(hbm, hbm, hbm),
+        scratch_shapes=[
+            pltpu.VMEM((CHUNKS, n_e, SLAB, oct_w), BF16),
+            pltpu.VMEM((OCT, toks, oct_w), BF16),
+            dma((CHUNKS,)),
+            dma((OCT,)),
+            dma((2, n_cut)),
+        ],
+        compiler_params=pltpu.CompilerParams(vmem_limit_bytes=60 * 2**20),
+    )(ids_row, back, gate_grad, up_grad)
     return token_grad, gate_grad[None], up_grad[None]
 
 

time: 292 us -> 498 us (1.71)
  Pallas kernels: 282 us -> 497 us
  local copies, waits for them, and re-layouts: 8.2 us -> 0 us
    pallas_call x1 -> x2, Pallas kernels: 282 us -> 497 us  [the longest x1 273 us: local(): pl.pallas_call(kernel, out_shape=(jax.ShapeDtypeStruct((CHUNKS, n_e, SLAB...]
    unnamed x7 -> x0, local copies, waits for them, and re-layouts: 8.2 us -> none
where the time goes in v3:
time: 498 us
  Pallas kernels  497 us (100%)
    pallas_call x1, Pallas kernels, local(): pl.pallas_call(kernel, out_shape=(jax.ShapeDtypeStruct((CHUNKS, n_e, SLAB...  273 us
    pallas_call x1, Pallas kernels, local(): pl.pallas_call(place, out_shape=(jax.ShapeDtypeStruct((toks, width), BF16...  224 us

profile of v3, /device:TPU:1, one launch (start us, length us, event | category | flops | bytes accessed | tf_op | source)
XLA Modules:
  0.0 497.7 jit_solution(11180891538507113623)
XLA Ops:
  0.6 272.6 %shard_map.94 = (bf16[3,32,16,896]{3,2,1,0:T(8,128)(2,1)}, bf16[7168,256]{1,0:T(8,128)(2,1)}, bf16[7168,256]{1,0:T(8,128)(2,1)}, bf16[2,2,2,32,7168]{4,3,2,1,0:T(8,128)(2,1)}) custom-call(s32[1,128]{1,0:T(1,128)} %bitcast.10, f32[1,128]{1,0:T(1,128)} %bitcast.12, bf16[128,7168]{1,0:T(8,128)(2,1)} %tok_hbm.1, bf16[128,7168]{1,0:T(8,128)(2,1)} %og_hbm.1, ...), custom_call_target="tpu_custom_call" | custom-call | tf_op jit(solution)/shard_map/pallas_call | solution.py:604
  273.3 224.3 %shard_map.95 = (bf16[128,7168]{1,0:T(8,128)(2,1)}, bf16[7168,256]{1,0:T(8,128)(2,1)}, bf16[7168,256]{1,0:T(8,128)(2,1)}) custom-call(s32[1,128]{1,0:T(1,128)} %bitcast.11, bf16[3,32,16,896]{3,2,1,0:T(8,128)(2,1)} %get-tuple-element.9.back_hbm, bf16[7168,256]{1,0:T(8,128)(2,1)} %get-tuple-element.10.gg_src, bf16[7168,256]{1,0:T(8,128)(2,1)} %get-tuple-element.11.ug_src), custom_call_target="tpu_custom_call" | custom-call | tf_op jit(solution)/shard_map/pallas_call | solution.py:664

commit v4 on v3

--- a/solution.py
+++ b/solution.py
@@ -11,7 +11,7 @@
 PER = 2
 OCT = 8
 SLAB = PER * OCT
-X, Y = 0, 1
+X, Y, Z = 0, 1, 2
 NN = (((1,), (0,)), ((), ()))
 NT = (((1,), (1,)), ((), ()))
 TN = (((0,), (0,)), ((), ()))
@@ -46,9 +46,9 @@
 
 def kernel(
     ids_ref, probs_ref, tok_hbm, og_hbm, wg_hbm, wu_hbm, wd_hbm,
-    back, gg_hbm, ug_hbm, fin_hbm,
-    tok, q, wg, wu, wd, wp, send, recv, rows, relay, fin, acc, part_acc, ex_out, ex_in, grads,
-    load_sem, disp_send, disp_recv, own_sem, ag_send, ag_recv, y_send, y_recv, w_send, w_recv,
+    back, gg_hbm, ug_hbm, fin_hbm, recv,
+    tok, q, wg, wu, wd, wp, send, slabs, ids_in, probs_in, rows, relay, fin, acc, part_acc, ex_out, ex_in, grads,
+    load_sem, disp_send, disp_recv, own_sem, ag_send, ag_recv, og_send, og_recv, meta_send, meta_recv, w_send, w_recv,
     ex_send, ex_recv, rs_send, rs_recv, ret_send, ret_recv, retown_sem, out_sem, fin_sem,
 ):
     n_x = lax.axis_size("dp")
@@ -66,6 +66,18 @@
     chunk_rows = n_x * n_e * PER
     log_half = half.bit_length() - 1
 
+    barrier = pltpu.get_barrier_semaphore()
+
+    def greet(d, carry):
+        pl.semaphore_signal(
+            barrier, inc=1, device_id=(me_x, lax.rem(me_e + d, n_e)), device_id_type=MESH
+        )
+        return carry
+
+    lax.fori_loop(1, n_e, greet, 0)
+    for x in nbr:
+        pl.semaphore_signal(barrier, inc=1, device_id=(x, me_e), device_id_type=MESH)
+
     loads = []
     for a, src in ((X, tok_hbm), (Y, og_hbm)):
         for j in range(OCT):
@@ -82,28 +94,55 @@
     for w in weights:
         w.start()
 
-    barrier = pltpu.get_barrier_semaphore()
-
-    def greet(d, carry):
-        pl.semaphore_signal(
-            barrier, inc=1, device_id=(me_x, lax.rem(me_e + d, n_e)), device_id_type=MESH
-        )
-        return carry
-
-    lax.fori_loop(1, n_e, greet, 0)
-    for x in nbr:
-        pl.semaphore_signal(barrier, inc=1, device_id=(x, me_e), device_id_type=MESH)
+    wide = width // 2
+
+    def swap_weight(i):
+        return pltpu.make_async_remote_copy(
+            src_ref=wd_hbm.at[:, pl.ds(i * wide, wide)],
+            dst_ref=wp.at[i],
+            send_sem=w_send.at[i],
+            recv_sem=w_recv.at[i],
+            device_id=(pair[i], me_e),
+            device_id_type=MESH,
+        )
+
+    def swap(src, dst, i, send_sem, recv_sem):
+        return pltpu.make_async_remote_copy(
+            src_ref=src,
+            dst_ref=dst,
+            send_sem=send_sem,
+            recv_sem=recv_sem,
+            device_id=(pair[1 - i], me_e),
+            device_id_type=MESH,
+        )
+
+    swaps = []
+    for i in range(2):
+        for n, (src, dst) in enumerate(((ids_ref, ids_in), (probs_ref, probs_in))):
+            swaps.append(swap(src, dst.at[i], i, meta_send.at[i, n], meta_recv.at[i, n]))
+    for j in range(OCT // 2):
+        for i in range(2):
+            at = i * (OCT // 2) + j
+            src = og_hbm.at[:, pl.ds(at * oct_w, oct_w)]
+            swaps.append(swap(src, tok.at[Z, at], i, og_send.at[at], og_recv.at[at]))
+
+    pl.semaphore_wait(barrier, n_e - 1 + 2)
+    for copy in swaps:
+        copy.start()
+    for i in range(2):
+        swap_weight(i).start()
 
     (rank_row, key_row), _ = slot_keys(ids_ref[...])
     probs = upright(probs_ref[...])
 
     n_slab_rows = n_e * SLAB
-    step = min(128, n_slab_rows)
-
-    def build_q(c):
-        keyc = jnp.where((rank_row >> 1) == c, key_row, -1)
+    step = min(256, n_slab_rows)
+
+    def build_q(c, keys=((rank_row, key_row),) * 2):
         i = iota((n_slab_rows, 1), 0)
         for j in range(OCT):
+            rank, key = keys[j // (OCT // 2)]
+            keyc = jnp.where((rank >> 1) == c, key, -1)
             want = jnp.where(((i >> 1) & (OCT - 1)) == j, (i >> 4) * PER + (i & 1), -2)
             q[:n_slab_rows, j * toks : (j + 1) * toks] = jnp.where(want == keyc, 1.0, 0.0).astype(BF16)
 
@@ -181,12 +220,16 @@
     def collect(a, c):
         pltpu.make_async_copy(send.at[a, c, me_e], recv.at[a, c, me_e], own_sem.at[a, c]).wait()
         dispatched(a, c).wait_recv()
+        load = pltpu.make_async_copy(recv.at[a, c], slabs, own_sem.at[a, c])
+        load.start()
+        load.wait()
         order = perm(iota((size, size), 0), iota((size, size), 1))
+        dst, block_at = (X, me_x) if a == X else (Y, me_x if a == Y else far)
         for h in range(2):
-            block = recv[a, c, h * gs : (h + 1) * gs].reshape(size, oct_w)
+            block = slabs[h * gs : (h + 1) * gs].reshape(size, oct_w)
             out = dot(order, block).astype(BF16)
             for j in range(OCT):
-                rows[a, c, me_x * 2 + h, :, j * oct_w : (j + 1) * oct_w] = out[
+                rows[dst, c, block_at * 2 + h, :, j * oct_w : (j + 1) * oct_w] = out[
                     j * half : (j + 1) * half
                 ]
 
@@ -196,34 +239,6 @@
         hop(X, c, me_x, 1, 1, 1).start()
         hop(X, c, me_x, 1, 0, 1).start()
         hop(X, c, me_x, 0, 1, 0).start()
-
-    wide = width // 2
-
-    def swap_weight(i):
-        return pltpu.make_async_remote_copy(
-            src_ref=wd_hbm.at[:, pl.ds(i * wide, wide)],
-            dst_ref=wp.at[i],
-            send_sem=w_send.at[i],
-            recv_sem=w_recv.at[i],
-            device_id=(pair[i], me_e),
-            device_id_type=MESH,
-        )
-
-    def lend(c, i, block):
-        ref = rows.at[Y, c, pl.ds(block * 2, 2), :, pl.ds(i * wide, wide)]
-        return pltpu.make_async_remote_copy(
-            src_ref=ref,
-            dst_ref=ref,
-            send_sem=y_send.at[c, i],
-            recv_sem=y_recv.at[c, i],
-            device_id=(pair[1 - i], me_e),
-            device_id_type=MESH,
-        )
-
-    def own_y(c):
-        collect(Y, c)
-        for i in range(2):
-            lend(c, i, me_x).start()
 
     def exchange(c, i):
         return pltpu.make_async_remote_copy(
@@ -281,7 +296,6 @@
 
     def partial(c):
         for i in range(2):
-            lend(c, i, pair[1 - i]).wait_recv()
             if c == 0:
                 swap_weight(i).wait_recv()
 
@@ -292,7 +306,7 @@
                 y = jnp.concatenate(
                     [
                         rows[Y, c, pl.ds(p * 2, 2), :, cols].reshape(block_rows, step_w)
-                        for p in (me_x, pair[1 - i])
+                        for p in (me_x, far)
                     ],
                     axis=0,
                 )
@@ -323,7 +337,6 @@
     def backward(c):
         for i in range(2):
             exchange(c, i).wait_recv()
-            lend(c, i, me_x).wait_send()
         for i in range(2):
             acc[2, pair[i]] += ex_in[c, i, :block_rows].astype(F32)
         acc[2, far] = ex_in[c, 0, block_rows:].astype(F32) + ex_in[c, 1, block_rows:].astype(F32)
@@ -479,55 +492,67 @@
             for copy in tile(i, i % 2):
                 copy.wait()
 
+    def fill_out(a, c):
+        fill(a, c)
+        dispatch(a, c)
+
     build_q(0)
-    pl.semaphore_wait(barrier, n_e - 1 + 2)
-    for i in range(2):
-        swap_weight(i).start()
     for copy in loads[:OCT]:
         copy.wait()
-    fill(X, 0)
-    dispatch(X, 0)
+    fill_out(X, 0)
     for copy in loads[OCT:]:
         copy.wait()
     for j in range(OCT):
         tok[Y, j] = (tok[Y, j].astype(F32) * probs).astype(BF16)
-    fill(Y, 0)
-    dispatch(Y, 0)
+    fill_out(Y, 0)
     build_q(1)
-    fill(X, 1)
-    dispatch(X, 1)
+    fill_out(X, 1)
+    fill_out(Y, 1)
+    for copy in swaps:
+        copy.wait_recv()
+    partner_keys = tuple(slot_keys(ids_in[i])[0] for i in range(2))
+    for j in range(OCT):
+        scale = upright(probs_in[j // (OCT // 2)])
+        tok[Z, j] = (tok[Z, j].astype(F32) * scale).astype(BF16)
+    build_q(0, partner_keys)
+    fill_out(Z, 0)
     own(0)
-    fill(Y, 1)
-    dispatch(Y, 1)
-    own_y(0)
     build_q(2)
-    for a in (X, Y):
-        fill(a, 2)
-        dispatch(a, 2)
-    arrive(0)
+    fill_out(X, 2)
+    build_q(1, partner_keys)
+    fill_out(Z, 1)
+    build_q(2)
+    fill_out(Y, 2)
+    build_q(2, partner_keys)
+    fill_out(Z, 2)
+    collect(Y, 0)
     for copy in weights:
         copy.wait()
     own(1)
-    own_y(1)
+    collect(Z, 0)
+    arrive(0)
+    collect(Y, 1)
+    partial(0)
+    own(2)
+    arrive(1)
     complete(0)
     forward(0)
-    partial(0)
-    arrive(1)
-    own(2)
-    own_y(2)
     backward(0)
     start_reduce(0)
+    collect(Z, 1)
+    partial(1)
+    arrive(2)
     complete(1)
     forward(1)
-    partial(1)
-    arrive(2)
     pass_on(0)
     backward(1)
     start_reduce(1)
+    collect(Y, 2)
+    collect(Z, 2)
+    partial(2)
     finish(0)
     complete(2)
     forward(2)
-    partial(2)
     pass_on(1)
     backward(2)
     start_reduce(2)
@@ -537,7 +562,8 @@
     finish(2)
     for c in range(CHUNKS):
         sent(c)
-        dispatched(Y, c).wait_send()
+        for a in (Y, Z):
+            dispatched(a, c).wait_send()
         for i in range(2):
             exchange(c, i).wait_send()
         for p in range(2):
@@ -548,43 +574,60 @@
         scattered(send.at[X, c], back.at[c], ret_send.at[c], ret_recv.at[c]).wait()
     for i in range(2):
         swap_weight(i).wait_send()
-
-
-def place(ids_ref, back_hbm, gg_src, ug_src, tg_hbm, gg_hbm, ug_hbm, back, out, back_sem, tg_sem, grad_sem):
+    for copy in swaps:
+        copy.wait_send()
+
+
+def place(ids_ref, back_hbm, gg_src, ug_src, tg_hbm, gg_hbm, ug_hbm, back, rows, out, grad, back_sem, tg_sem, in_sem, out_sem):
     width = gg_src.shape[0]
     n_e = back.shape[1]
     oct_w = back.shape[3]
-    n_cut = grad_sem.shape[1]
-    cut = width // n_cut
+    cut = width // (OCT // 2)
     came = [pltpu.make_async_copy(back_hbm.at[c], back.at[c], back_sem.at[c]) for c in range(CHUNKS)]
-    moves = [
-        pltpu.make_async_copy(
-            src.at[pl.ds(i * cut, cut)], dst.at[pl.ds(i * cut, cut)], grad_sem.at[o, i]
-        )
-        for i in range(n_cut)
-        for o, (src, dst) in enumerate(((gg_src, gg_hbm), (ug_src, ug_hbm)))
-    ]
-    for copy in came + moves:
+    moves = []
+    for j in range(OCT):
+        o, at = j % 2, pl.ds((j // 2) * cut, cut)
+        src, dst = ((gg_src, gg_hbm), (ug_src, ug_hbm))[o]
+        moves.append(
+            (
+                pltpu.make_async_copy(src.at[at], grad.at[o, at], in_sem.at[j]),
+                pltpu.make_async_copy(grad.at[o, at], dst.at[at], out_sem.at[j]),
+            )
+        )
+    for copy in came:
+        copy.start()
+    for copy, _ in moves:
         copy.start()
     _, (rank_col, key_col) = slot_keys(ids_ref[...])
-    i = iota((1, n_e * SLAB), 1)
-    for copy in came:
-        copy.wait()
+    half = n_e // 2 * SLAB
+    per_half = n_e // 2 * PER
+    slot, col = iota((half, half), 0), iota((half, half), 1)
+    j, rest = slot // per_half, slot % per_half
+    order = jnp.where(col == (rest // PER) * SLAB + j * PER + rest % PER, 1.0, 0.0).astype(BF16)
+    at = (rank_col // PER) * (n_e * PER) + key_col
+    here = jnp.where(at == iota((1, CHUNKS * n_e * PER), 1), 1.0, 0.0).astype(BF16)
+    for c in range(CHUNKS):
+        came[c].wait()
+        for h in range(2):
+            block = back[c, h * (n_e // 2) : (h + 1) * (n_e // 2)].reshape(half, oct_w)
+            flat = dot(order, block).astype(BF16)
+            first = c * n_e * PER + h * per_half
+            for j in range(OCT):
+                rows[first : first + per_half, j * oct_w : (j + 1) * oct_w] = flat[
+                    j * per_half : (j + 1) * per_half
+                ]
     outs = []
     for j in range(OCT):
-        want = jnp.where(((i >> 1) & (OCT - 1)) == j, (i >> 4) * PER + (i & 1), -2)
-        total = None
-        for c in range(CHUNKS):
-            keyc = jnp.where((rank_col >> 1) == c, key_col, -1)
-            here = jnp.where(keyc == want, 1.0, 0.0).astype(BF16)
-            one = dot(here, back[c].reshape(n_e * SLAB, oct_w))
-            total = one if total is None else total + one
-        out[j] = total.astype(BF16)
+        out[j] = dot(here, rows[:, j * oct_w : (j + 1) * oct_w]).astype(BF16)
         outs.append(
             pltpu.make_async_copy(out.at[j], tg_hbm.at[:, pl.ds(j * oct_w, oct_w)], tg_sem.at[j])
         )
         outs[-1].start()
-    for copy in outs + moves:
+        moves[j][0].wait()
+        moves[j][1].start()
+    for copy in outs:
+        copy.wait()
+    for _, copy in moves:
         copy.wait()
 
 
@@ -601,25 +644,28 @@
     hbm = pl.BlockSpec(memory_space=pl.ANY)
     dma = pltpu.SemaphoreType.DMA
     ids_row = expert_ids.reshape(1, toks)
-    back, gate_grad, up_grad, _ = pl.pallas_call(
+    back, gate_grad, up_grad, _, _ = pl.pallas_call(
         kernel,
         out_shape=(
             jax.ShapeDtypeStruct((CHUNKS, n_e, SLAB, oct_w), BF16),
             jax.ShapeDtypeStruct((width, quarter), BF16),
             jax.ShapeDtypeStruct((width, quarter), BF16),
             jax.ShapeDtypeStruct((CHUNKS - 1, 2, 2, n_e, width), BF16),
+            jax.ShapeDtypeStruct((3, CHUNKS, n_e, SLAB, oct_w), BF16),
         ),
         in_specs=[vmem] * 2 + [hbm] * 5,
-        out_specs=(hbm, hbm, hbm, hbm),
+        out_specs=(hbm,) * 5,
         scratch_shapes=[
-            pltpu.VMEM((2, OCT, toks, oct_w), BF16),
+            pltpu.VMEM((3, OCT, toks, oct_w), BF16),
             pltpu.VMEM((max(n_e * SLAB, bw), max(OCT * toks, 4 * quarter)), BF16),
             pltpu.VMEM((width, quarter), BF16),
             pltpu.VMEM((width, quarter), BF16),
             pltpu.VMEM((quarter, width), BF16),
             pltpu.VMEM((2, quarter, width // 2), BF16),
-            pltpu.VMEM((2, CHUNKS, n_e, SLAB, oct_w), BF16),
-            pltpu.VMEM((2, CHUNKS, n_e, SLAB, oct_w), BF16),
+            pltpu.VMEM((3, CHUNKS, n_e, SLAB, oct_w), BF16),
+            pltpu.VMEM((n_e, SLAB, oct_w), BF16),
+            pltpu.VMEM((2, 1, toks), jnp.int32),
+            pltpu.VMEM((2, 1, toks), F32),
             pltpu.VMEM((2, CHUNKS, 2 * n_x, n_e, width), BF16),
             pltpu.VMEM((CHUNKS, 2, n_e, width), BF16),
             pltpu.VMEM((2, 2, n_e, width), BF16),
@@ -629,13 +675,15 @@
             pltpu.VMEM((CHUNKS, 2, 2 * n_e * PER, quarter), BF16),
             pltpu.VMEM((CHUNKS * chunk_rows, 2 * quarter), BF16),
             dma((3, OCT)),
-            dma((2, CHUNKS)),
-            dma((2, CHUNKS)),
-            dma((2, CHUNKS)),
+            dma((3, CHUNKS)),
+            dma((3, CHUNKS)),
+            dma((3, CHUNKS)),
             dma((CHUNKS, 2, 3)),
             dma((CHUNKS, 2, 3)),
-            dma((CHUNKS, 2)),
-            dma((CHUNKS, 2)),
+            dma((OCT,)),
+            dma((OCT,)),
+            dma((2, 2)),
+            dma((2, 2)),
             dma((2,)),
             dma((2,)),
             dma((CHUNKS, 2)),
@@ -660,7 +708,6 @@
         up_w,
         down_w,
     )
-    n_cut = 4
     token_grad, gate_grad, up_grad = pl.pallas_call(
         place,
         out_shape=(
@@ -672,10 +719,13 @@
         out_specs=(hbm, hbm, hbm),
         scratch_shapes=[
             pltpu.VMEM((CHUNKS, n_e, SLAB, oct_w), BF16),
+            pltpu.VMEM((CHUNKS * n_e * PER, width), BF16),
             pltpu.VMEM((OCT, toks, oct_w), BF16),
+            pltpu.VMEM((2, width, quarter), BF16),
             dma((CHUNKS,)),
             dma((OCT,)),
-            dma((2, n_cut)),
+            dma((OCT,)),
+            dma((OCT,)),
         ],
         compiler_params=pltpu.CompilerParams(vmem_limit_bytes=60 * 2**20),
     )(ids_row, back, gate_grad, up_grad)

time: 498 us -> 273 us (0.55)
  Pallas kernels: 497 us -> 271 us
    pallas_call x1, Pallas kernels: 224 us -> 8.6 us  [local(): pl.pallas_call(place, out_shape=(jax.ShapeDtypeStruct((toks, width), BF16...]
    pallas_call x1, Pallas kernels: 273 us -> 263 us  [local(): pl.pallas_call(kernel, out_shape=(jax.ShapeDtypeStruct((CHUNKS, n_e, SLAB...]
where the time goes in v4:
time: 273 us; the launch traced here: 272 us
  Pallas kernels  271 us (99%)
    pallas_call x1, Pallas kernels, local(): pl.pallas_call(kernel, out_shape=(jax.ShapeDtypeStruct((CHUNKS, n_e, SLAB...  263 us
    pallas_call x1, Pallas kernels, local(): pl.pallas_call(place, out_shape=(jax.ShapeDtypeStruct((toks, width), BF16...  8.6 us

profile of v4, /device:TPU:1, one launch (start us, length us, event | category | flops | bytes accessed | tf_op | source)
XLA Modules:
  0.0 272.3 jit_solution(6836392408904026667)
XLA Ops:
  0.6 262.9 %shard_map.94 = (bf16[3,32,16,896]{3,2,1,0:T(8,128)(2,1)}, bf16[7168,256]{1,0:T(8,128)(2,1)}, bf16[7168,256]{1,0:T(8,128)(2,1)}, bf16[2,2,2,32,7168]{4,3,2,1,0:T(8,128)(2,1)}, bf16[3,3,32,16,896]{4,3,2,1,0:T(8,128)(2,1)}) custom-call(s32[1,128]{1,0:T(1,128)} %bitcast.10, f32[1,128]{1,0:T(1,128)} %bitcast.12, bf16[128,7168]{1,0:T(8,128)(2,1)} %tok_hbm.1, ...), custom_call_target="tpu_custom_call" | custom-call | tf_op jit(solution)/shard_map/pallas_call | solution.py:647
  263.5 8.6 %shard_map.95 = (bf16[128,7168]{1,0:T(8,128)(2,1)}, bf16[7168,256]{1,0:T(8,128)(2,1)}, bf16[7168,256]{1,0:T(8,128)(2,1)}) custom-call(s32[1,128]{1,0:T(1,128)} %bitcast.11, bf16[3,32,16,896]{3,2,1,0:T(8,128)(2,1)} %get-tuple-element.9.back_hbm, bf16[7168,256]{1,0:T(8,128)(2,1)} %get-tuple-element.10.gg_src, bf16[7168,256]{1,0:T(8,128)(2,1)} %get-tuple-element.11.ug_src), custom_call_target="tpu_custom_call" | custom-call | tf_op jit(solution)/shard_map/pallas_call | solution.py:711

commit v5 on v4

--- a/solution.py
+++ b/solution.py
@@ -11,7 +11,8 @@
 PER = 2
 OCT = 8
 SLAB = PER * OCT
-X, Y, Z = 0, 1, 2
+X, Y, Z, V = 0, 1, 2, 3
+SOURCE = (0, 0, 1, 2)
 NN = (((1,), (0,)), ((), ()))
 NT = (((1,), (1,)), ((), ()))
 TN = (((0,), (0,)), ((), ()))
@@ -48,7 +49,7 @@
     ids_ref, probs_ref, tok_hbm, og_hbm, wg_hbm, wu_hbm, wd_hbm,
     back, gg_hbm, ug_hbm, fin_hbm, recv,
     tok, q, wg, wu, wd, wp, send, slabs, ids_in, probs_in, rows, relay, fin, acc, part_acc, ex_out, ex_in, grads,
-    load_sem, disp_send, disp_recv, own_sem, ag_send, ag_recv, og_send, og_recv, meta_send, meta_recv, w_send, w_recv,
+    load_sem, disp_send, disp_recv, own_sem, ag_send, ag_recv, raw_send, raw_recv, meta_send, meta_recv, w_send, w_recv,
     ex_send, ex_recv, rs_send, rs_recv, ret_send, ret_recv, retown_sem, out_sem, fin_sem,
 ):
     n_x = lax.axis_size("dp")
@@ -78,15 +79,15 @@
     for x in nbr:
         pl.semaphore_signal(barrier, inc=1, device_id=(x, me_e), device_id_type=MESH)
 
-    loads = []
-    for a, src in ((X, tok_hbm), (Y, og_hbm)):
-        for j in range(OCT):
-            loads.append(
-                pltpu.make_async_copy(
-                    src.at[:, pl.ds(j * oct_w, oct_w)], tok.at[a, j], load_sem.at[a, j]
-                )
-            )
-            loads[-1].start()
+    loads = [
+        pltpu.make_async_copy(
+            src.at[:, pl.ds(j * oct_w, oct_w)], tok.at[SOURCE[a], j], load_sem.at[a, j]
+        )
+        for a, src in ((X, tok_hbm), (Y, og_hbm))
+        for j in range(OCT)
+    ]
+    for copy in loads[:OCT]:
+        copy.start()
     weights = [
         pltpu.make_async_copy(src, dst, load_sem.at[2, i])
         for i, (src, dst) in enumerate(((wg_hbm, wg), (wu_hbm, wu), (wd_hbm, wd)))
@@ -120,11 +121,15 @@
     for i in range(2):
         for n, (src, dst) in enumerate(((ids_ref, ids_in), (probs_ref, probs_in))):
             swaps.append(swap(src, dst.at[i], i, meta_send.at[i, n], meta_recv.at[i, n]))
-    for j in range(OCT // 2):
-        for i in range(2):
-            at = i * (OCT // 2) + j
-            src = og_hbm.at[:, pl.ds(at * oct_w, oct_w)]
-            swaps.append(swap(src, tok.at[Z, at], i, og_send.at[at], og_recv.at[at]))
+    for a, whole in ((V, tok_hbm), (Z, og_hbm)):
+        for j in range(OCT // 2):
+            for i in range(2):
+                at = i * (OCT // 2) + j
+                src = whole.at[:, pl.ds(at * oct_w, oct_w)]
+                n = a - Z
+                dst = tok.at[SOURCE[a], at]
+                swaps.append(swap(src, dst, i, raw_send.at[n, at], raw_recv.at[n, at]))
+    first_cotangent = len(swaps) - OCT
 
     pl.semaphore_wait(barrier, n_e - 1 + 2)
     for copy in swaps:
@@ -139,18 +144,26 @@
     step = min(256, n_slab_rows)
 
     def build_q(c, keys=((rank_row, key_row),) * 2):
-        i = iota((n_slab_rows, 1), 0)
-        for j in range(OCT):
-            rank, key = keys[j // (OCT // 2)]
-            keyc = jnp.where((rank >> 1) == c, key, -1)
-            want = jnp.where(((i >> 1) & (OCT - 1)) == j, (i >> 4) * PER + (i & 1), -2)
-            q[:n_slab_rows, j * toks : (j + 1) * toks] = jnp.where(want == keyc, 1.0, 0.0).astype(BF16)
+        for part, (rank, key) in enumerate(keys):
+
+            def body(j, carry):
+                keyc = jnp.where((rank >> 1) == c, key, -1)
+                i = iota((n_slab_rows, 1), 0)
+                want = jnp.where(((i >> 1) & (OCT - 1)) == j, (i >> 4) * PER + (i & 1), -2)
+                cols = pl.ds(pl.multiple_of(j * toks, toks), toks)
+                q[:n_slab_rows, cols] = jnp.where(want == keyc, 1.0, 0.0).astype(BF16)
+                return carry
+
+            lax.fori_loop(part * (OCT // 2), (part + 1) * (OCT // 2), body, 0)
+
+    def slab_of(a, c):
+        return send.at[((Y, 2), (Z, 1), (Z, 2))[c] if a == V else (a, c)]
 
     def fill(a, c):
         def body(m, carry):
             part = q[pl.ds(pl.multiple_of(m * step, step), step), : OCT * toks]
-            out = dot(part, tok[a].reshape(OCT * toks, oct_w)).astype(BF16)
-            send[a, c, pl.ds(m * (step // SLAB), step // SLAB)] = out.reshape(
+            out = dot(part, tok[SOURCE[a]].reshape(OCT * toks, oct_w)).astype(BF16)
+            slab_of(a, c)[pl.ds(m * (step // SLAB), step // SLAB)] = out.reshape(
                 step // SLAB, SLAB, oct_w
             )
             return carry
@@ -186,20 +199,20 @@
 
     def dispatch(a, c):
         scatter(
-            send.at[a, c], recv.at[a, c], disp_send.at[a, c], disp_recv.at[a, c], own_sem.at[a, c]
+            slab_of(a, c), recv.at[a, c], disp_send.at[a, c], disp_recv.at[a, c], own_sem.at[a, c]
         )
 
     def dispatched(a, c):
-        return scattered(send.at[a, c], recv.at[a, c], disp_send.at[a, c], disp_recv.at[a, c])
-
-    def hop(a, c, block, h, way, slot):
-        ref = rows.at[a, c, block * 2 + h]
+        return scattered(slab_of(a, c), recv.at[a, c], disp_send.at[a, c], disp_recv.at[a, c])
+
+    def share(c, i, n, block):
+        ref = rows.at[X, c, pl.ds(block * 2, 2), :, pl.ds(i * wide, wide)]
         return pltpu.make_async_remote_copy(
             src_ref=ref,
             dst_ref=ref,
-            send_sem=ag_send.at[c, way, slot],
-            recv_sem=ag_recv.at[c, way, slot],
-            device_id=(nbr[way], me_e),
+            send_sem=ag_send.at[c, i, n],
+            recv_sem=ag_recv.at[c, i, n],
+            device_id=(pair[i], me_e),
             device_id_type=MESH,
         )
 
@@ -218,27 +231,33 @@
         return jnp.where(col == (rest >> 1) * SLAB + j * PER + (rest & 1), 1.0, 0.0).astype(BF16)
 
     def collect(a, c):
-        pltpu.make_async_copy(send.at[a, c, me_e], recv.at[a, c, me_e], own_sem.at[a, c]).wait()
+        pltpu.make_async_copy(slab_of(a, c).at[me_e], recv.at[a, c, me_e], own_sem.at[a, c]).wait()
         dispatched(a, c).wait_recv()
         load = pltpu.make_async_copy(recv.at[a, c], slabs, own_sem.at[a, c])
         load.start()
         load.wait()
         order = perm(iota((size, size), 0), iota((size, size), 1))
-        dst, block_at = (X, me_x) if a == X else (Y, me_x if a == Y else far)
+        dst = X if a in (X, V) else Y
+        block_at = {X: (me_x, me_x), Y: (me_x, me_x), Z: (far, far), V: (pair[1], pair[0])}[a]
         for h in range(2):
             block = slabs[h * gs : (h + 1) * gs].reshape(size, oct_w)
             out = dot(order, block).astype(BF16)
             for j in range(OCT):
-                rows[dst, c, block_at * 2 + h, :, j * oct_w : (j + 1) * oct_w] = out[
+                rows[
+                    dst, c, block_at[j // (OCT // 2)] * 2 + h, :, j * oct_w : (j + 1) * oct_w
+                ] = out[
                     j * half : (j + 1) * half
                 ]
 
     def own(c):
         collect(X, c)
-        hop(X, c, me_x, 0, 0, 0).start()
-        hop(X, c, me_x, 1, 1, 1).start()
-        hop(X, c, me_x, 1, 0, 1).start()
-        hop(X, c, me_x, 0, 1, 0).start()
+        for i in range(2):
+            share(c, i, 0, me_x).start()
+
+    def lent(c):
+        collect(V, c)
+        for i in range(2):
+            share(c, i, 1, pair[1 - i]).start()
 
     def exchange(c, i):
         return pltpu.make_async_remote_copy(
@@ -250,22 +269,15 @@
             device_id_type=MESH,
         )
 
-    def arrive(c):
-        for way in range(2):
-            block = nbr[1 - way]
-            hop(X, c, block, way, way, way).wait_recv()
-            hop(X, c, block, way, way, 2).start()
-
     def complete(c):
-        for way in range(2):
-            hop(X, c, nbr[1 - way], 1 - way, way, 1 - way).wait_recv()
-            hop(X, c, far, way, way, 2).wait_recv()
+        for i in range(2):
+            share(c, i, 0, pair[i]).wait_recv()
+            share(c, i, 1, far).wait_recv()
 
     def sent(c):
-        for way in range(2):
-            for slot in range(2):
-                hop(X, c, me_x, slot, way, slot).wait_send()
-            hop(X, c, nbr[1 - way], way, way, 2).wait_send()
+        for i in range(2):
+            share(c, i, 0, me_x).wait_send()
+            share(c, i, 1, pair[1 - i]).wait_send()
 
     kw = width // 4
 
@@ -311,17 +323,17 @@
                     axis=0,
                 )
                 mine = dot(y, wd[:, cols], NT)
-                lent = dot(y, wp[i, :, near], NT)
+                other = dot(y, wp[i, :, near], NT)
 
                 @pl.when(k == 0)
                 def _():
                     part_acc[0] = mine
-                    part_acc[1] = lent
+                    part_acc[1] = other
 
                 @pl.when(k > 0)
                 def _():
                     part_acc[0] += mine
-                    part_acc[1] += lent
+                    part_acc[1] += other
 
                 return carry
 
@@ -496,63 +508,77 @@
         fill(a, c)
         dispatch(a, c)
 
-    build_q(0)
     for copy in loads[:OCT]:
         copy.wait()
-    fill_out(X, 0)
+    for c in range(CHUNKS):
+        build_q(c)
+        fill(X, c)
+        if c < 2:
+            dispatch(X, c)
+    for copy in loads[OCT:]:
+        copy.start()
+    for copy in swaps[:first_cotangent]:
+        copy.wait_recv()
+    partner_keys = tuple(slot_keys(ids_in[i])[0] for i in range(2))
+    for c in range(2):
+        build_q(c, partner_keys)
+        fill_out(V, c)
     for copy in loads[OCT:]:
         copy.wait()
     for j in range(OCT):
-        tok[Y, j] = (tok[Y, j].astype(F32) * probs).astype(BF16)
+        tok[SOURCE[Y], j] = (tok[SOURCE[Y], j].astype(F32) * probs).astype(BF16)
+    build_q(0)
     fill_out(Y, 0)
-    build_q(1)
-    fill_out(X, 1)
-    fill_out(Y, 1)
-    for copy in swaps:
+    for copy in swaps[first_cotangent:]:
         copy.wait_recv()
-    partner_keys = tuple(slot_keys(ids_in[i])[0] for i in range(2))
     for j in range(OCT):
         scale = upright(probs_in[j // (OCT // 2)])
-        tok[Z, j] = (tok[Z, j].astype(F32) * scale).astype(BF16)
+        tok[SOURCE[Z], j] = (tok[SOURCE[Z], j].astype(F32) * scale).astype(BF16)
     build_q(0, partner_keys)
     fill_out(Z, 0)
+    dispatch(X, 2)
+    build_q(2, partner_keys)
+    fill_out(V, 2)
+    build_q(1)
+    fill_out(Y, 1)
     own(0)
-    build_q(2)
-    fill_out(X, 2)
+    own(1)
+    lent(0)
+    lent(1)
+    for c in range(2):
+        dispatched(V, c).wait_send()
     build_q(1, partner_keys)
     fill_out(Z, 1)
     build_q(2)
     fill_out(Y, 2)
+    for copy in weights:
+        copy.wait()
+    collect(Y, 0)
+    collect(Z, 0)
+    partial(0)
+    own(2)
+    complete(0)
+    forward(0)
+    lent(2)
+    dispatched(V, 2).wait_send()
     build_q(2, partner_keys)
     fill_out(Z, 2)
-    collect(Y, 0)
-    for copy in weights:
-        copy.wait()
-    own(1)
-    collect(Z, 0)
-    arrive(0)
-    collect(Y, 1)
-    partial(0)
-    own(2)
-    arrive(1)
-    complete(0)
-    forward(0)
     backward(0)
     start_reduce(0)
+    collect(Y, 1)
+    complete(1)
+    forward(1)
     collect(Z, 1)
     partial(1)
-    arrive(2)
-    complete(1)
-    forward(1)
     pass_on(0)
     backward(1)
     start_reduce(1)
+    complete(2)
+    forward(2)
     collect(Y, 2)
     collect(Z, 2)
     partial(2)
     finish(0)
-    complete(2)
-    forward(2)
     pass_on(1)
     backward(2)
     start_reduce(2)
@@ -651,7 +677,7 @@
             jax.ShapeDtypeStruct((width, quarter), BF16),
             jax.ShapeDtypeStruct((width, quarter), BF16),
             jax.ShapeDtypeStruct((CHUNKS - 1, 2, 2, n_e, width), BF16),
-            jax.ShapeDtypeStruct((3, CHUNKS, n_e, SLAB, oct_w), BF16),
+            jax.ShapeDtypeStruct((4, CHUNKS, n_e, SLAB, oct_w), BF16),
         ),
         in_specs=[vmem] * 2 + [hbm] * 5,
         out_specs=(hbm,) * 5,
@@ -675,13 +701,13 @@
             pltpu.VMEM((CHUNKS, 2, 2 * n_e * PER, quarter), BF16),
             pltpu.VMEM((CHUNKS * chunk_rows, 2 * quarter), BF16),
             dma((3, OCT)),
-            dma((3, CHUNKS)),
-            dma((3, CHUNKS)),
-            dma((3, CHUNKS)),
-            dma((CHUNKS, 2, 3)),
-            dma((CHUNKS, 2, 3)),
-            dma((OCT,)),
-            dma((OCT,)),
+            dma((4, CHUNKS)),
+            dma((4, CHUNKS)),
+            dma((4, CHUNKS)),
+            dma((CHUNKS, 2, 2)),
+            dma((CHUNKS, 2, 2)),
+            dma((2, OCT)),
+            dma((2, OCT)),
             dma((2, 2)),
             dma((2, 2)),
             dma((2,)),

time: 273 us -> 263 us (0.963)
  Pallas kernels: 271 us -> 262 us
    pallas_call x1, Pallas kernels: 263 us -> 253 us  [local(): pl.pallas_call(kernel, out_shape=(jax.ShapeDtypeStruct((CHUNKS, n_e, SLAB...]
where the time goes in v5:
time: 263 us
  Pallas kernels  262 us (100%)
    pallas_call x1, Pallas kernels, local(): pl.pallas_call(kernel, out_shape=(jax.ShapeDtypeStruct((CHUNKS, n_e, SLAB...  253 us
    pallas_call x1, Pallas kernels, local(): pl.pallas_call(place, out_shape=(jax.ShapeDtypeStruct((toks, width), BF16...  8.6 us

profile of v5, /device:TPU:1, one launch (start us, length us, event | category | flops | bytes accessed | tf_op | source)
XLA Modules:
  0.0 262.6 jit_solution(13918368426180074909)
XLA Ops:
  0.6 253.2 %shard_map.94 = (bf16[3,32,16,896]{3,2,1,0:T(8,128)(2,1)}, bf16[7168,256]{1,0:T(8,128)(2,1)}, bf16[7168,256]{1,0:T(8,128)(2,1)}, bf16[2,2,2,32,7168]{4,3,2,1,0:T(8,128)(2,1)}, bf16[4,3,32,16,896]{4,3,2,1,0:T(8,128)(2,1)}) custom-call(s32[1,128]{1,0:T(1,128)} %bitcast.10, f32[1,128]{1,0:T(1,128)} %bitcast.12, bf16[128,7168]{1,0:T(8,128)(2,1)} %tok_hbm.1, ...), custom_call_target="tpu_custom_call" | custom-call | tf_op jit(solution)/shard_map/pallas_call | solution.py:673
  253.8 8.6 %shard_map.95 = (bf16[128,7168]{1,0:T(8,128)(2,1)}, bf16[7168,256]{1,0:T(8,128)(2,1)}, bf16[7168,256]{1,0:T(8,128)(2,1)}) custom-call(s32[1,128]{1,0:T(1,128)} %bitcast.11, bf16[3,32,16,896]{3,2,1,0:T(8,128)(2,1)} %get-tuple-element.9.back_hbm, bf16[7168,256]{1,0:T(8,128)(2,1)} %get-tuple-element.10.gg_src, bf16[7168,256]{1,0:T(8,128)(2,1)} %get-tuple-element.11.ug_src), custom_call_target="tpu_custom_call" | custom-call | tf_op jit(solution)/shard_map/pallas_call | solution.py:737

commit v6 on v5

--- a/solution.py
+++ b/solution.py
@@ -583,8 +583,8 @@
     backward(2)
     start_reduce(2)
     finish(1)
+    weight_grads()
     pass_on(2)
-    weight_grads()
     finish(2)
     for c in range(CHUNKS):
         sent(c)
@@ -642,6 +642,9 @@
                 rows[first : first + per_half, j * oct_w : (j + 1) * oct_w] = flat[
                     j * per_half : (j + 1) * per_half
                 ]
+        for came_in, go_out in moves[(0, 2, 5)[c] : (2, 5, 8)[c]]:
+            came_in.wait()
+            go_out.start()
     outs = []
     for j in range(OCT):
         out[j] = dot(here, rows[:, j * oct_w : (j + 1) * oct_w]).astype(BF16)
@@ -649,8 +652,6 @@
             pltpu.make_async_copy(out.at[j], tg_hbm.at[:, pl.ds(j * oct_w, oct_w)], tg_sem.at[j])
         )
         outs[-1].start()
-        moves[j][0].wait()
-        moves[j][1].start()
     for copy in outs:
         copy.wait()
     for _, copy in moves:

time: 263 us -> 261 us (level)
  no operation moved by 1% of the time
where the time goes in v6:
time: 261 us; the launch traced here: 260 us
  Pallas kernels  260 us (100%)
    pallas_call x1, Pallas kernels, local(): pl.pallas_call(kernel, out_shape=(jax.ShapeDtypeStruct((CHUNKS, n_e, SLAB...  252 us
    pallas_call x1, Pallas kernels, local(): pl.pallas_call(place, out_shape=(jax.ShapeDtypeStruct((toks, width), BF16...  7.42 us

profile of v6, /device:TPU:1, one launch (start us, length us, event | category | flops | bytes accessed | tf_op | source)
XLA Modules:
  0.0 260.4 jit_solution(16543193897776260487)
XLA Ops:
  0.6 252.1 %shard_map.94 = (bf16[3,32,16,896]{3,2,1,0:T(8,128)(2,1)}, bf16[7168,256]{1,0:T(8,128)(2,1)}, bf16[7168,256]{1,0:T(8,128)(2,1)}, bf16[2,2,2,32,7168]{4,3,2,1,0:T(8,128)(2,1)}, bf16[4,3,32,16,896]{4,3,2,1,0:T(8,128)(2,1)}) custom-call(s32[1,128]{1,0:T(1,128)} %bitcast.10, f32[1,128]{1,0:T(1,128)} %bitcast.12, bf16[128,7168]{1,0:T(8,128)(2,1)} %tok_hbm.1, ...), custom_call_target="tpu_custom_call" | custom-call | tf_op jit(solution)/shard_map/pallas_call | solution.py:674
  252.8 7.4 %shard_map.95 = (bf16[128,7168]{1,0:T(8,128)(2,1)}, bf16[7168,256]{1,0:T(8,128)(2,1)}, bf16[7168,256]{1,0:T(8,128)(2,1)}) custom-call(s32[1,128]{1,0:T(1,128)} %bitcast.11, bf16[3,32,16,896]{3,2,1,0:T(8,128)(2,1)} %get-tuple-element.9.back_hbm, bf16[7168,256]{1,0:T(8,128)(2,1)} %get-tuple-element.10.gg_src, bf16[7168,256]{1,0:T(8,128)(2,1)} %get-tuple-element.11.ug_src), custom_call_target="tpu_custom_call" | custom-call | tf_op jit(solution)/shard_map/pallas_call | solution.py:738

commit v7 on v6

--- a/solution.py
+++ b/solution.py
@@ -458,15 +458,16 @@
                 for i in range(gs // 2):
                     send[X, c, h * gs + 2 * i + p] = out[i * SLAB : (i + 1) * SLAB]
 
-            def body(d, carry):
-                give_back(c, lax.rem(me_e // 2 + d, n_e // 2) * 2 + p)
-                return carry
-
-            lax.fori_loop(1, n_e // 2, body, 0)
-
-            @pl.when(lax.rem(me_e, 2) != p)
-            def _():
-                give_back(c, (me_e // 2) * 2 + p)
+                def body(d, carry):
+                    peer = h * gs + lax.rem(me_e // 2 + d, gs // 2) * 2 + p
+
+                    @pl.when(peer != me_e)
+                    def _():
+                        give_back(c, peer)
+
+                    return carry
+
+                lax.fori_loop(0, gs // 2, body, 0)
 
         pltpu.make_async_copy(send.at[X, c, me_e], back.at[c, me_e], retown_sem.at[c]).start()
 

time: 261 us -> 261 us (level)
  no operation moved by 1% of the time
where the time goes in v7:
time: 261 us; the launch traced here: 260 us
  Pallas kernels  259 us (99%)
    pallas_call x1, Pallas kernels, local(): pl.pallas_call(kernel, out_shape=(jax.ShapeDtypeStruct((CHUNKS, n_e, SLAB...  252 us
    pallas_call x1, Pallas kernels, local(): pl.pallas_call(place, out_shape=(jax.ShapeDtypeStruct((toks, width), BF16...  7.42 us

profile of v7, /device:TPU:1, one launch (start us, length us, event | category | flops | bytes accessed | tf_op | source)
XLA Modules:
  0.0 259.7 jit_solution(768901908426815281)
XLA Ops:
  0.6 251.5 %shard_map.94 = (bf16[3,32,16,896]{3,2,1,0:T(8,128)(2,1)}, bf16[7168,256]{1,0:T(8,128)(2,1)}, bf16[7168,256]{1,0:T(8,128)(2,1)}, bf16[2,2,2,32,7168]{4,3,2,1,0:T(8,128)(2,1)}, bf16[4,3,32,16,896]{4,3,2,1,0:T(8,128)(2,1)}) custom-call(s32[1,128]{1,0:T(1,128)} %bitcast.10, f32[1,128]{1,0:T(1,128)} %bitcast.12, bf16[128,7168]{1,0:T(8,128)(2,1)} %tok_hbm.1, ...), custom_call_target="tpu_custom_call" | custom-call | tf_op jit(solution)/shard_map/pallas_call | solution.py:675
  252.2 7.4 %shard_map.95 = (bf16[128,7168]{1,0:T(8,128)(2,1)}, bf16[7168,256]{1,0:T(8,128)(2,1)}, bf16[7168,256]{1,0:T(8,128)(2,1)}) custom-call(s32[1,128]{1,0:T(1,128)} %bitcast.11, bf16[3,32,16,896]{3,2,1,0:T(8,128)(2,1)} %get-tuple-element.9.back_hbm, bf16[7168,256]{1,0:T(8,128)(2,1)} %get-tuple-element.10.gg_src, bf16[7168,256]{1,0:T(8,128)(2,1)} %get-tuple-element.11.ug_src), custom_call_target="tpu_custom_call" | custom-call | tf_op jit(solution)/shard_map/pallas_call | solution.py:739
